TPU v7x, 32 devices: a whole 2x2x4 slice. The times are simulated.
32 devices in a mesh: space: 8 (over y, x, core), freq: 4 (over z).
Axes of the slice: x: 2, y: 2, z: 4, core: 2. Of those that a mesh axis runs over, the one named last changes fastest.
Arguments:
- snapshots: bfloat16 [32768, 1024], P('space', 'freq'), may hold values from -6 to 6
- tail: bfloat16 [32768, 128], P('space'), may hold values from -6 to 6
Outputs:
- gram: float32 [16, 2, 8, 8], P('freq', None, 'space')
- spectrum: float32 [16], P('freq')
All inputs are finite; a program needn't handle non-finite values.
Results may differ from a plain program's by a relative error of at most 0.0038.
Values may be sent and summed in bfloat16 or wider, within the bound.
A program may use at most 64 MiB of HBM per device.

v0:
```python
import math

import jax
import jax.numpy as jnp
from jax import lax
from jax.sharding import PartitionSpec as P

FREQ_DEV = 4
NFFT = 256
POWER = 4


def shifted(value, axis, steps):
    count = lax.axis_size(axis)
    initial, last = (max(0, -steps), min(count, count - steps))
    return lax.ppermute(value, axis, [(source, source + steps) for source in range(initial, last)])


def build_table(count):
    steps = jnp.arange(NFFT, dtype=jnp.int32)
    freqs = jnp.arange(count, dtype=jnp.int32)
    window = 0.5 - 0.5 * jnp.cos(2.0 * math.pi * steps.astype(jnp.float32) / NFFT)
    phase = 2.0 * math.pi * (steps[:, None] * freqs[None, :] % NFFT).astype(jnp.float32) / NFFT
    table = jnp.concatenate(
        [window[:, None] * jnp.cos(phase), -window[:, None] * jnp.sin(phase)], 1
    )
    return (table.astype(jnp.bfloat16), jnp.sum(window * window))


def transform(extended, table):
    points, width = extended.shape
    half = NFFT // 2
    count = width // half - 1
    halves = extended.reshape(points, count + 1, half)
    blocks = jnp.concatenate([halves[:, :-1], halves[:, 1:]], 2)
    coef = jnp.einsum("pbt,tk->bkp", blocks, table, preferred_element_type=jnp.float32)
    return coef.reshape(count, 2, table.shape[1] // 2, points).astype(jnp.bfloat16)


def gram_terms(coef, scale):
    big = jnp.einsum("bcfp,gdfp->fcbdg", coef, coef, preferred_element_type=jnp.float32)
    real = big[:, 0, :, 0, :] + big[:, 1, :, 1, :]
    imag = big[:, 0, :, 1, :] - big[:, 1, :, 0, :]
    return jnp.stack([real, imag], 1) * scale


def apply_matrix(matrix, vector):
    high = lax.Precision.HIGHEST
    m_real, m_imag = (matrix[:, 0], matrix[:, 1])
    v_real, v_imag = (vector[:, 0], vector[:, 1])
    u_real = jnp.einsum("fjk,fk->fj", m_real, v_real, precision=high) - jnp.einsum(
        "fjk,fk->fj", m_imag, v_imag, precision=high
    )
    u_imag = jnp.einsum("fjk,fk->fj", m_real, v_imag, precision=high) + jnp.einsum(
        "fjk,fk->fj", m_imag, v_real, precision=high
    )
    return jnp.stack([u_real, u_imag], 1)


def rescale(product):
    return product / jnp.sqrt(jnp.mean(product * product, axis=(1, 2), keepdims=True) + 1e-06)


def rayleigh(vector, product):
    return jnp.mean(vector * product, axis=(1, 2)) / (
        jnp.mean(vector * vector, axis=(1, 2)) + 1e-06
    )


def shards(snapshots, tail):
    points = snapshots.shape[0]
    freq_count = lax.axis_size("freq")
    half = NFFT // 2
    table, wsum = build_table(FREQ_DEV * freq_count)
    scale = 1.0 / (points * lax.axis_size("space") * wsum)
    following = shifted(snapshots[:, :half], "freq", -1)
    is_last = lax.axis_index("freq") == freq_count - 1
    following = jnp.where(is_last, tail, following)
    extended = jnp.concatenate([snapshots, following], 1)
    coef = transform(extended, table)
    regrouped = lax.all_to_all(coef, "freq", split_axis=2, concat_axis=0, tiled=True)
    partial_value = gram_terms(regrouped, scale)
    blocks_all = partial_value.shape[2]
    held = blocks_all // lax.axis_size("space")
    vector = jnp.stack(
        [
            jnp.ones((FREQ_DEV, blocks_all), jnp.float32),
            jnp.zeros((FREQ_DEV, blocks_all), jnp.float32),
        ],
        1,
    )
    total = lax.psum(partial_value, "space")
    for step in range(POWER):
        vector = rescale(apply_matrix(total, vector))
    spectrum = rayleigh(vector, apply_matrix(total, vector))
    gram_rows = lax.dynamic_slice_in_dim(total, lax.axis_index("space") * held, held, 2)
    return (gram_rows, spectrum)


def solution(mesh):
    in_specs = (P("space", "freq"), P("space", None))
    out_specs = (P("freq", None, "space", None), P("freq"))
    return jax.shard_map(shards, mesh=mesh, in_specs=in_specs, out_specs=out_specs, check_vma=False)
```

profile of v0, /device:TPU:0, one launch (start us, length us, event | category | flops | bytes accessed | tf_op | source)
XLA Modules:
  0.0 96.6 jit_solution(8692053492315397055)
XLA Ops:
  0.6 2.9 %copy.19 = bf16[4096,256]{0,1:T(8,128)(2,1)S(1)} copy(bf16[4096,256]{1,0:T(8,128)(2,1)} %param.2) | data formatting | bytes 4194304 | tf_op args[0]
  3.6 1.1 %slice.76 = bf16[4096,128]{0,1:T(8,128)(2,1)} slice(bf16[4096,256]{0,1:T(8,128)(2,1)S(1)} %copy.19), slice={[0:4096], [0:128]} | slice | bytes 2097152 | tf_op jit(solution)/shard_map/slice | solution.py:76
  4.6 1.3 %collective-permute-start = (bf16[4096,128]{0,1:T(8,128)(2,1)}, bf16[4096,128]{0,1:T(8,128)(2,1)}, u32[]{:S(2)}, u32[]{:S(2)}) collective-permute-start(bf16[4096,128]{0,1:T(8,128)(2,1)} %slice.76), channel_id=1, source_target_pairs={{1,0},{2,1},{3,2},{5,4},{6,5},{7,6},{9,8},{10,9},{11,10},{13,12},{... | collective-permute-start | bytes 3145736 | tf_op jit(solution)/shard_map/ppermute | solution.py:16
  5.9 1.5 %copy.18 = bf16[4096,128]{0,1:T(8,128)(2,1)S(1)} copy(bf16[4096,128]{1,0:T(8,128)(2,1)} %param.3) | data formatting | bytes 2097152 | tf_op args[1]
  7.6 25.4 %collective-permute-done = bf16[4096,128]{0,1:T(8,128)(2,1)} collective-permute-done((bf16[4096,128]{0,1:T(8,128)(2,1)}, bf16[4096,128]{0,1:T(8,128)(2,1)}, u32[]{:S(2)}, u32[]{:S(2)}) %collective-permute-start) | collective-permute-done | bytes 1048608 | tf_op jit(solution)/shard_map/ppermute | solution.py:16
  33.0 1.3 %broadcast_select_fusion = bf16[4096,128]{0,1:T(8,128)(2,1)S(1)} fusion(bf16[4096,128]{0,1:T(8,128)(2,1)S(1)} %copy.18, bf16[4096,128]{0,1:T(8,128)(2,1)} %collective-permute-done, pred[]{:T(512)S(6)} %eq.5), kind=kLoop, calls=%fused_computation.6 | loop fusion | flops 524288 | bytes 3145729 | tf_op jit(solution)/shard_map/jit(_where)/select_n | solution.py:78
  34.3 0.2 pad_maximum_fusion
  34.6 1.8 %fusion.43 = (bf16[4096,2,128]{0,2,1:T(8,128)(2,1)}, bf16[4096,2,128]{0,2,1:T(8,128)(2,1)S(1)}) fusion(bf16[4096,3,128]{0,2,1:T(8,128)(2,1)S(1)} %bitcast.173), kind=kLoop, calls=%fused_computation.88 | loop fusion | bytes 8388608 | tf_op jit(solution)/shard_map/slice | solution.py:35
  36.4 4.1 %copy.59 = bf16[4096,2,128]{2,0,1:T(8,128)(2,1)} copy(bf16[4096,2,128]{0,2,1:T(8,128)(2,1)} %get-tuple-element.10) | data formatting | bytes 4194304
  40.5 2.5 %copy.60 = bf16[4096,2,128]{2,0,1:T(8,128)(2,1)} copy(bf16[4096,2,128]{0,2,1:T(8,128)(2,1)S(1)} %get-tuple-element.11) | data formatting | bytes 4194304
  42.9 3.5 %convolution_convert_fusion = bf16[32,4096,2]{1,0,2:T(8,128)(2,1)S(1)} fusion(bf16[4096,2,128]{2,0,1:T(8,128)(2,1)} %copy.60, bf16[4096,2,128]{2,0,1:T(8,128)(2,1)} %copy.59, bf16[256,16]{0,1:T(8,128)(2,1)S(1)} %get-tuple-element.20, bf16[256,16]{0,1:T(8,128)(2,1)S(1)} %get-tuple-element.21), kind=kOutput, calls=%fused_computation | convolution fusion | flops 142901248 | bytes 4734976 | tf_op jit(solution)/shard_map/pbt,tk->bkp/dot_general | solution.py:36
  46.5 1.3 %copy.22 = bf16[2,2,16,4096]{3,1,0,2:T(2,128)(2,1)} copy(bf16[2,2,16,4096]{3,2,1,0:T(8,128)(2,1)S(1)} %bitcast.176) | data formatting | bytes 1048576 | tf_op jit(solution)/shard_map/convert_element_type | solution.py:37
  47.8 4.0 %all-to-all-start = ((bf16[2,2,16,4096]{3,1,0,2:T(2,128)(2,1)}), bf16[2,2,16,4096]{3,1,0,2:T(2,128)(2,1)S(1)}, u32[]{:S(2)}, u32[]{:S(2)}) async-start(bf16[2,2,16,4096]{3,1,0,2:T(2,128)(2,1)} %copy.22), calls=%async_computation | async-start | bytes 1048576 | tf_op jit(solution)/shard_map/all_to_all | solution.py:81
  51.8 0.6 multiply_reduce_fusion.5
  53.2 12.3 %all-to-all-done = bf16[2,2,16,4096]{3,1,0,2:T(2,128)(2,1)S(1)} async-done(((bf16[2,2,16,4096]{3,1,0,2:T(2,128)(2,1)}), bf16[2,2,16,4096]{3,1,0,2:T(2,128)(2,1)S(1)}, u32[]{:S(2)}, u32[]{:S(2)}) %all-to-all-start) | async-done | bytes 524320 | tf_op jit(solution)/shard_map/all_to_all | solution.py:81
  65.5 0.6 copy.64
  66.1 0.2 reshape.91
  66.3 1.2 %convolution_bitcast_fusion = f32[4,2,8,2,8]{2,4,1,3,0:T(8,128)S(1)} fusion(bf16[8,2,4,4096,1]{3,0,1,2,4:T(8,128)(2,1)S(1)} %reshape.91), kind=kOutput, calls=%fused_computation.5 | convolution fusion | flops 8388608 | bytes 528384 | tf_op jit(solution)/shard_map/bcfp,gdfp->fcbdg/dot_general | solution.py:41
  67.6 23.3 %psum.7 = f32[4,2,8,8]{2,3,0,1:T(8,128)S(1)} all-reduce(f32[4,2,8,8]{2,3,0,1:T(8,128)S(1)} %maximum_multiply_fusion), channel_id=1, replica_groups=mesh['space'=8,'freq'=4] {'space'}, use_global_device_ids=true, to_apply=%region_1.2 | all-reduce | flops 512 | bytes 4096 | tf_op jit(solution)/shard_map/psum | solution.py:92
  91.0 0.2 fusion.24
  91.2 0.2 fusion.25
  91.3 0.2 fusion.34
  91.7 0.2 fusion.23
  92.0 0.2 fusion.33
  92.6 0.2 fusion.21
  92.8 0.2 fusion.30
  93.5 0.2 fusion.19
  94.0 0.2 fusion.18
  94.4 0.2 fusion.17
  95.1 0.7 copy.26
  95.8 0.2 fusion.36
  96.0 0.5 add_divide_fusion
  (45 shorter events, 2.8 us)
Async XLA Ops:
  4.6 28.4 %collective-permute-start = (bf16[4096,128]{0,1:T(8,128)(2,1)}, bf16[4096,128]{0,1:T(8,128)(2,1)}, u32[]{:S(2)}, u32[]{:S(2)}) collective-permute-start(bf16[4096,128]{0,1:T(8,128)(2,1)} %slice.76), channel_id=1, source_target_pairs={{1,0},{2,1},{3,2},{5,4},{6,5},{7,6},{9,8},{10,9},{11,10},{13,12},{... | collective-permute-start | bytes 3145736 | tf_op jit(solution)/shard_map/ppermute | solution.py:16
  47.8 17.7 %all-to-all-start = ((bf16[2,2,16,4096]{3,1,0,2:T(2,128)(2,1)}), bf16[2,2,16,4096]{3,1,0,2:T(2,128)(2,1)S(1)}, u32[]{:S(2)}, u32[]{:S(2)}) async-start(bf16[2,2,16,4096]{3,1,0,2:T(2,128)(2,1)} %copy.22), calls=%async_computation | async-start | bytes 1048576 | tf_op jit(solution)/shard_map/all_to_all | solution.py:81
where the time goes:
time: 97 us; the launch traced here: 96.6 us
  waiting for transfers between devices  37.7 us (39%)
  blocking collectives  23.3 us (24%)
  local copies, waits for them, and re-layouts  16.7 us (17%)
  matrix products  8.05 us (8%)
  starting transfers between devices  5.3 us (5%)
  other arithmetic  4.01 us (4%)
  between operations  1.49 us (2%)
    ppermute x1, waiting for transfers between devices, shifted(): lax.ppermute(value, axis, [(source, source + steps) for source in range(i...  25.4 us
    psum x1, blocking collectives, shards(): total = lax.psum(partial_value, 'space')  23.3 us
    all_to_all x1, waiting for transfers between devices, shards(): lax.all_to_all(coef, 'freq', split_axis=2, concat_axis=0, tiled=True)  12.3 us
    unnamed x5, local copies, waits for them, and re-layouts  11.7 us
    all_to_all x1, starting transfers between devices, shards(): lax.all_to_all(coef, 'freq', split_axis=2, concat_axis=0, tiled=True)  4.02 us
    dot_general x1, matrix products, transform(): jnp.einsum('pbt,tk->bkp', blocks, table, preferred_element_type=jnp.float32)  3.53 us
  transfers between devices with their start and end apart: 2, of which 2 were waited for; matrix products, arithmetic and copies ran while one was open for 2% of the time, Pallas kernels for 0%

commit v1 on v0

--- a/solution.py
+++ b/solution.py
@@ -1,13 +1,21 @@
+import functools
 import math
 
 import jax
 import jax.numpy as jnp
+import ml_dtypes
+import numpy as np
 from jax import lax
+from jax.experimental import pallas as pl
+from jax.experimental.pallas import tpu as pltpu
 from jax.sharding import PartitionSpec as P
 
 FREQ_DEV = 4
 NFFT = 256
 POWER = 4
+LANES = 128
+SUBS = 2
+MESH = pl.DeviceIdType.MESH
 
 
 def shifted(value, axis, steps):
@@ -67,7 +75,7 @@
     )
 
 
-def shards(snapshots, tail):
+def shards_general(snapshots, tail):
     points = snapshots.shape[0]
     freq_count = lax.axis_size("freq")
     half = NFFT // 2
@@ -97,6 +105,360 @@
     return (gram_rows, spectrum)
 
 
+def two_pieces(values):
+    high = values.astype(ml_dtypes.bfloat16)
+    low = (values - high.astype(np.float64)).astype(ml_dtypes.bfloat16)
+    return np.concatenate([high, low], 0)
+
+
+def half_rows(nf):
+    steps = np.arange(NFFT // 2)
+    phase = 2.0 * np.pi * (np.arange(nf + 1)[:, None] * steps[None, :] % NFFT) / NFFT
+    real, imag = np.cos(phase), -np.sin(phase)
+    main = np.concatenate([real[:nf], imag[:nf]], 0)
+    main[nf] = real[nf]
+    return main, imag[nf : nf + 1]
+
+
+def make_tables(nf, pieces):
+    main, extra = half_rows(nf)
+    half = NFFT // 2
+    width = 2 * nf
+    both = np.zeros((2 * width + 2 * pieces, NFFT))
+    for h in range(2):
+        both[h * width : (h + 1) * width, h * half : (h + 1) * half] = main
+        both[2 * width + h :: 2, h * half : (h + 1) * half] = extra
+    last = np.zeros((width + 16, half))
+    last[:width] = main
+    last[width] = extra[0]
+    return two_pieces(both), two_pieces(last)
+
+
+def make_combine(nf, nb, pieces):
+    width = 2 * nf
+    main_rows = nb * width
+    ext_rows = nb * pieces
+    combine = np.zeros((2, nf, nb, main_rows + ext_rows + width + 16))
+
+    def columns(m, f, part):
+        if f == nf and part == 1:
+            if m == nb:
+                return [main_rows + ext_rows + width]
+            first = main_rows + m // 2 * 2 * pieces + m % 2
+            return [first + 2 * q for q in range(pieces)]
+        start = main_rows + ext_rows if m == nb else m * width
+        if f == nf:
+            return [start + nf]
+        if part == 1 and f == 0:
+            return []
+        return [start + part * nf + f]
+
+    for f in range(nf):
+        for b in range(nb):
+            for m in (b, b + 1):
+                second = m - b
+                sign = (-1.0) ** f if second else 1.0
+                side = 0.25 if second else -0.25
+                for part in range(2):
+                    for g, weight in ((f, 0.5), (f - 1, side), (f + 1, side)):
+                        flip = -1.0 if g < 0 and part == 1 else 1.0
+                        for column in columns(m, abs(g), part):
+                            combine[part, f, b, column] += sign * flip * weight
+    return combine.reshape(2 * nf * nb, -1).astype(ml_dtypes.bfloat16)
+
+
+def xor_index(index, other, count):
+    result = 0
+    bit = 1
+    while bit < count:
+        digit = lax.rem(index // bit, 2)
+        result = result + bit * ((1 - digit) if other & bit else digit)
+        bit *= 2
+    return result
+
+
+def nt_dot(left, right):
+    return lax.dot_general(
+        left, right, (((1,), (1,)), ((), ())), preferred_element_type=jnp.float32
+    )
+
+
+def leading_value(g_re, g_im, nb):
+    shape = g_re.shape
+    row = lax.broadcasted_iota(jnp.int32, shape, 0)
+    lane = lax.broadcasted_iota(jnp.int32, shape, 1)
+    entries = 2.0 * nb
+
+    def lane_sum(x):
+        step = 1
+        while step < nb:
+            ahead = pltpu.roll(x, LANES - step, 1)
+            behind = pltpu.roll(x, step, 1)
+            x = x + jnp.where(lane % (2 * step) < step, ahead, behind)
+            step *= 2
+        return x
+
+    def row_sum(x):
+        return jnp.broadcast_to(jnp.sum(x, axis=0, keepdims=True), shape)
+
+    def to_lanes(v_re, v_im):
+        return row_sum(g_re * v_re + g_im * v_im), row_sum(g_re * v_im - g_im * v_re)
+
+    def to_rows(v_re, v_im):
+        return lane_sum(g_re * v_re - g_im * v_im), lane_sum(g_re * v_im + g_im * v_re)
+
+    v_re, v_im = jnp.ones(shape, jnp.float32), jnp.zeros(shape, jnp.float32)
+    for step in range(POWER):
+        if step % 2 == 0:
+            u_re, u_im = to_lanes(v_re, v_im)
+            mean = lane_sum(u_re * u_re + u_im * u_im) / entries
+        else:
+            u_re, u_im = to_rows(v_re, v_im)
+            mean = row_sum(u_re * u_re + u_im * u_im) / entries
+        size = jnp.sqrt(mean + 1e-06)
+        v_re, v_im = u_re / size, u_im / size
+    u_re, u_im = to_lanes(v_re, v_im)
+    here = lane % nb == row
+    across_re = row_sum(jnp.where(here, v_re, 0.0))
+    across_im = row_sum(jnp.where(here, v_im, 0.0))
+    top = lane_sum(across_re * u_re + across_im * u_im) / entries
+    return top / (row_sum(v_re * v_re + v_im * v_im) / entries + 1e-06)
+
+
+def kernel(
+    zs, ns, nf, nb, scale,
+    snap_ref, tail_ref, table_ref, tail_table_ref, combine_ref, out_ref,
+    x_buf, tail_buf, table, tail_table, combine,
+    send, send_ext, recv, recv_ext, z_part, z_recv, s_recv,
+    x_sem, const_sem, send_sem, recv_sem, ext_send_sem, ext_recv_sem,
+    z_send_sem, z_recv_sem, s_send_sem, s_recv_sem,
+):
+    my_s, my_z = lax.axis_index("space"), lax.axis_index("freq")
+    quarter = snap_ref.shape[0] // zs
+    sub = quarter // SUBS
+    width = 2 * nf
+    pieces = sub // LANES
+    order = list(range(zs // 2, zs)) + list(range(1, zs // 2))
+    peers = {k: xor_index(my_z, k, zs) for k in order}
+    peers[0] = my_z
+    friends = {k: xor_index(my_s, k, ns) for k in range(1, ns)}
+
+    loads = {}
+    constants = [
+        pltpu.make_async_copy(table_ref, table, const_sem.at[0]),
+        pltpu.make_async_copy(tail_table_ref, tail_table, const_sem.at[1]),
+        pltpu.make_async_copy(combine_ref, combine, const_sem.at[2]),
+        pltpu.make_async_copy(
+            tail_ref.at[pl.ds(pl.multiple_of(my_z * quarter, quarter), quarter)],
+            tail_buf, const_sem.at[3],
+        ),
+    ]
+    constants[0].start()
+    for s in range(SUBS):
+        for k in order + [0]:
+            first = pl.multiple_of(peers[k] * quarter + s * sub, sub)
+            loads[k, s] = pltpu.make_async_copy(
+                snap_ref.at[pl.ds(first, sub)], x_buf.at[k, s], x_sem.at[k, s]
+            )
+            loads[k, s].start()
+    for copy in constants[1:]:
+        copy.start()
+
+    barrier = pltpu.get_barrier_semaphore()
+    for k in order:
+        pl.semaphore_signal(barrier, inc=1, device_id=(my_s, peers[k]), device_id_type=MESH)
+    for k in range(1, ns):
+        pl.semaphore_signal(barrier, inc=1, device_id=(friends[k], my_z), device_id_type=MESH)
+
+    ext_row = lax.broadcasted_iota(jnp.int32, (2 * pieces, LANES), 0) // 2
+
+    def transform(k, s):
+        loads[k, s].wait()
+        both = nt_dot(table[...], x_buf[k, s])
+        rows = both.shape[0] // 2
+        both = both[:rows] + both[rows:]
+        extra = jnp.zeros((2 * pieces, LANES), jnp.float32)
+        for q in range(pieces):
+            extra = jnp.where(
+                ext_row == q, both[2 * width :, q * LANES : (q + 1) * LANES], extra
+            )
+        return both[: 2 * width].astype(jnp.bfloat16), extra
+
+    constants[0].wait()
+    copies = {}
+    for s in range(SUBS):
+        for k in order:
+            main, extra = transform(k, s)
+            send[k, s] = main
+            send_ext[k, s] = extra
+            if s == 0 and k == order[0]:
+                pl.semaphore_wait(barrier, zs - 1 + ns - 1)
+            target = (my_s, peers[k])
+            copies[k, s] = [
+                pltpu.make_async_remote_copy(
+                    send_ext.at[k, s], recv_ext.at[my_z, s],
+                    ext_send_sem.at[k, s], ext_recv_sem.at[k, s],
+                    device_id=target, device_id_type=MESH,
+                ),
+                pltpu.make_async_remote_copy(
+                    send.at[k, s], recv.at[my_z, s],
+                    send_sem.at[k, s], recv_sem.at[k, s],
+                    device_id=target, device_id_type=MESH,
+                ),
+            ]
+            for copy in copies[k, s]:
+                copy.start()
+    for s in range(SUBS):
+        main, extra = transform(0, s)
+        recv[my_z, s] = main
+        recv_ext[my_z, s] = extra
+    for copy in constants[1:]:
+        copy.wait()
+
+    gram = jnp.zeros((width * nb, width * nb), jnp.float32)
+    for s in range(SUBS):
+        last = nt_dot(tail_table[...], tail_buf[s * sub : (s + 1) * sub])
+        rows = last.shape[0] // 2
+        last = (last[:rows] + last[rows:]).astype(jnp.bfloat16)
+        for k in order:
+            for copy in copies[k, s]:
+                copy.wait_recv()
+        extras = []
+        for d in range(zs):
+            extra = recv_ext[d, s]
+            extras.append(
+                jnp.concatenate([jnp.where(ext_row == q, extra, 0.0) for q in range(pieces)], 1)
+            )
+        stacked = jnp.concatenate(
+            [recv[d, s] for d in range(zs)]
+            + [jnp.concatenate(extras, 0).astype(jnp.bfloat16), last],
+            0,
+        )
+        coef = jnp.dot(combine[...], stacked, preferred_element_type=jnp.float32)
+        coef = coef.astype(jnp.bfloat16)
+        gram = gram + nt_dot(coef, coef)
+
+    side = nf * nb
+    real = gram[:side, :side] + gram[side:, side:]
+    imag = gram[:side, side:] - gram[side:, :side]
+    lane_freq = lax.broadcasted_iota(jnp.int32, (nb, side), 1) // nb
+    g_re = jnp.zeros((nb, side), jnp.float32)
+    g_im = jnp.zeros((nb, side), jnp.float32)
+    for f in range(nf):
+        g_re = jnp.where(lane_freq == f, real[f * nb : (f + 1) * nb], g_re)
+        g_im = jnp.where(lane_freq == f, imag[f * nb : (f + 1) * nb], g_im)
+    z_part[0] = g_re * scale
+    z_part[1] = g_im * scale
+
+    z_copies = []
+    for k in order:
+        copy = pltpu.make_async_remote_copy(
+            z_part, z_recv.at[k], z_send_sem.at[k], z_recv_sem.at[k],
+            device_id=(my_s, peers[k]), device_id_type=MESH,
+        )
+        copy.start()
+        z_copies.append(copy)
+    total = z_part[...]
+    for k, copy in zip(order, z_copies):
+        copy.wait_recv()
+        total = total + z_recv[k]
+    s_recv[my_s] = total
+    s_copies = []
+    for k in range(1, ns):
+        copy = pltpu.make_async_remote_copy(
+            s_recv.at[my_s], s_recv.at[my_s], s_send_sem.at[k], s_recv_sem.at[k],
+            device_id=(friends[k], my_z), device_id_type=MESH,
+        )
+        copy.start()
+        s_copies.append(copy)
+    for copy in s_copies:
+        copy.wait_recv()
+    total = s_recv[0]
+    for d in range(1, ns):
+        total = total + s_recv[d]
+    g_re, g_im = total[0], total[1]
+
+    value = leading_value(g_re, g_im, nb)
+    row = lax.broadcasted_iota(jnp.int32, (nb, side), 0)
+    mine = row == my_s
+    row_re = jnp.sum(jnp.where(mine, g_re, 0.0), axis=0, keepdims=True)
+    row_im = jnp.sum(jnp.where(mine, g_im, 0.0), axis=0, keepdims=True)
+    result = jnp.where(row == 0, row_re, jnp.where(row == 1, row_im, value))
+    group = FREQ_DEV * nb
+    placed = result
+    for z in range(1, zs):
+        placed = jnp.where(my_z == z, pltpu.roll(result, LANES - z * group, 1), placed)
+    out_ref[...] = placed
+
+    for group_copies in copies.values():
+        for copy in group_copies:
+            copy.wait_send()
+    for copy in z_copies + s_copies:
+        copy.wait_send()
+
+
+def shards_kernel(zs, ns, snapshots, tail):
+    points, steps = snapshots.shape
+    nf = FREQ_DEV * zs
+    nb = 2 * zs
+    sub = points // zs // SUBS
+    pieces = sub // LANES
+    width = 2 * nf
+    table, tail_table = make_tables(nf, pieces)
+    combine = make_combine(nf, nb, pieces)
+    window = 0.5 - 0.5 * np.cos(2.0 * np.pi * np.arange(NFFT) / NFFT)
+    scale = float(1.0 / (points * ns * np.sum(window * window)))
+    dma = pltpu.SemaphoreType.DMA
+    flops = 2 * points * steps * table.shape[0]
+    packed = pl.pallas_call(
+        functools.partial(kernel, zs, ns, nf, nb, scale),
+        out_shape=jax.ShapeDtypeStruct((nb, LANES), jnp.float32),
+        in_specs=[pl.BlockSpec(memory_space=pl.ANY)] * 5,
+        out_specs=pl.BlockSpec(memory_space=pltpu.VMEM),
+        scratch_shapes=[
+            pltpu.VMEM((zs, SUBS, sub, steps), jnp.bfloat16),
+            pltpu.VMEM((points // zs, tail.shape[1]), jnp.bfloat16),
+            pltpu.VMEM(table.shape, jnp.bfloat16),
+            pltpu.VMEM(tail_table.shape, jnp.bfloat16),
+            pltpu.VMEM(combine.shape, jnp.bfloat16),
+            pltpu.VMEM((zs, SUBS, 2 * width, sub), jnp.bfloat16),
+            pltpu.VMEM((zs, SUBS, 2 * pieces, LANES), jnp.float32),
+            pltpu.VMEM((zs, SUBS, 2 * width, sub), jnp.bfloat16),
+            pltpu.VMEM((zs, SUBS, 2 * pieces, LANES), jnp.float32),
+            pltpu.VMEM((2, nb, LANES), jnp.float32),
+            pltpu.VMEM((zs, 2, nb, LANES), jnp.float32),
+            pltpu.VMEM((ns, 2, nb, LANES), jnp.float32),
+            dma((zs, SUBS)), dma((4,)),
+            dma((zs, SUBS)), dma((zs, SUBS)), dma((zs, SUBS)), dma((zs, SUBS)),
+            dma((zs,)), dma((zs,)), dma((ns,)), dma((ns,)),
+        ],
+        compiler_params=pltpu.CompilerParams(
+            collective_id=0, has_side_effects=True, vmem_limit_bytes=32 * 1024 * 1024
+        ),
+        cost_estimate=pl.CostEstimate(
+            flops=flops, bytes_accessed=points * steps * 2, transcendentals=0
+        ),
+    )(snapshots, tail, jnp.asarray(table), jnp.asarray(tail_table), jnp.asarray(combine))
+    group = FREQ_DEV * nb
+    rows = packed[:2, :group].reshape(2, FREQ_DEV, 1, nb).transpose(1, 0, 2, 3)
+    return rows, packed[2, :group:nb]
+
+
+def power_of_two(count):
+    return count > 1 and count & (count - 1) == 0
+
+
+def shards(snapshots, tail):
+    zs, ns = lax.axis_size("freq"), lax.axis_size("space")
+    points, steps = snapshots.shape
+    nb = zs * steps // (NFFT // 2)
+    packs = FREQ_DEV * zs * nb == LANES and steps == NFFT and nb == ns == 8
+    whole = points % (zs * SUBS * LANES * 4) == 0
+    if packs and whole and power_of_two(zs) and power_of_two(ns):
+        return shards_kernel(zs, ns, snapshots, tail)
+    return shards_general(snapshots, tail)
+
+
 def solution(mesh):
     in_specs = (P("space", "freq"), P("space", None))
     out_specs = (P("freq", None, "space", None), P("freq"))

time: 97 us -> 36.2 us (0.37)
  waiting for transfers between devices: 37.7 us -> 0 us
  Pallas kernels: 0 us -> 28.6 us
  blocking collectives: 23.3 us -> 0 us
  local copies, waits for them, and re-layouts: 16.7 us -> 6.64 us
  matrix products: 8.05 us -> 0 us
  starting transfers between devices: 5.3 us -> 0 us
  other arithmetic: 4.01 us -> 0 us
    pallas_call x0 -> x1, Pallas kernels: none -> 28.6 us  [shards_kernel(): pl.pallas_call(functools.partial(kernel, zs, ns, nf, nb, scale), out_shap...]
    ppermute x1 -> x0, waiting for transfers between devices: 25.4 us -> none  [shifted(): lax.ppermute(value, axis, [(source, source + steps) for source in range(i...]
    psum x1 -> x0, blocking collectives: 23.3 us -> none  [shards(): total = lax.psum(partial_value, 'space')]
    all_to_all x1 -> x0, waiting for transfers between devices: 12.3 us -> none  [shards(): lax.all_to_all(coef, 'freq', split_axis=2, concat_axis=0, tiled=True)]
    dot_general x22 -> x0, matrix products: 8.05 us -> none  [the longest x1 3.53 us: transform(): jnp.einsum('pbt,tk->bkp', blocks, table, preferred_element_type=jnp.float32)]
    unnamed x5 -> x11, local copies, waits for them, and re-layouts: 11.7 us -> 5.96 us
    all_to_all x1 -> x0, starting transfers between devices: 4.02 us -> none  [shards(): lax.all_to_all(coef, 'freq', split_axis=2, concat_axis=0, tiled=True)]
    slice x6 -> x2, local copies, waits for them, and re-layouts: 2.88 us -> 0.6 us  [the longest x1 0.59 us: shards_kernel(): return (rows, packed[2, :group:nb])]
  transfers between devices with their start and end apart: 2 -> 0, of which waited for: 2 -> 0; matrix products, arithmetic and copies ran while one was open for 2% -> 0% of each run, Pallas kernels for 0% -> 0%
where the time goes in v1:
time: 36.2 us; the launch traced here: 35.9 us
  Pallas kernels  28.6 us (79%)
  local copies, waits for them, and re-layouts  6.64 us (18%)
  between operations  0.65 us (2%)
    pallas_call x1, Pallas kernels, shards_kernel(): pl.pallas_call(functools.partial(kernel, zs, ns, nf, nb, scale), out_shap...  28.6 us
    unnamed x11, local copies, waits for them, and re-layouts  5.96 us

profile of v1, /device:TPU:0, one launch (start us, length us, event | category | flops | bytes accessed | tf_op | source)
XLA Modules:
  0.0 35.9 jit_solution(18026456242970096243)
XLA Ops:
  0.6 0.0 copy-start
  0.6 1.6 %copy-done = bf16[4096,256]{1,0:T(8,128)(2,1)S(1)} copy-done((bf16[4096,256]{1,0:T(8,128)(2,1)S(1)}, bf16[4096,256]{1,0:T(8,128)(2,1)}, u32[]{:S(2)}) %copy-start) | copy-done | bytes 2097176
  2.2 0.0 copy-start.1
  2.2 1.2 %copy-done.1 = bf16[4096,128]{1,0:T(8,128)(2,1)S(1)} copy-done((bf16[4096,128]{1,0:T(8,128)(2,1)S(1)}, bf16[4096,128]{1,0:T(8,128)(2,1)}, u32[]{:S(2)}) %copy-start.1) | copy-done | bytes 1048600
  3.4 0.0 copy-start.2
  3.4 0.9 %copy-done.2 = bf16[256,336]{1,0:T(8,128)(2,1)S(1)} copy-done((bf16[256,336]{1,0:T(8,128)(2,1)S(1)}, bf16[256,336]{1,0:T(8,128)(2,1)}, u32[]{:S(2)}) %copy-start.2) | copy-done | bytes 172056
  4.4 0.0 copy-start.3
  4.4 0.9 %copy-done.3 = bf16[144,256]{1,0:T(8,128)(2,1)S(1)} copy-done((bf16[144,256]{1,0:T(8,128)(2,1)S(1)}, bf16[144,256]{1,0:T(8,128)(2,1)}, u32[]{:S(2)}) %copy-start.3) | copy-done | bytes 73752
  5.3 0.0 copy-start.4
  5.3 0.7 %copy-done.4 = bf16[96,128]{1,0:T(8,128)(2,1)S(1)} copy-done((bf16[96,128]{1,0:T(8,128)(2,1)S(1)}, bf16[96,128]{1,0:T(8,128)(2,1)}, u32[]{:S(2)}) %copy-start.4) | copy-done | bytes 24600
  6.0 28.6 %shard_map.68 = f32[8,128]{1,0:T(8,128)S(1)} custom-call(bf16[4096,256]{1,0:T(8,128)(2,1)S(1)} %copy-done, bf16[4096,128]{1,0:T(8,128)(2,1)S(1)} %copy-done.1, bf16[144,256]{1,0:T(8,128)(2,1)S(1)} %copy-done.3, bf16[96,128]{1,0:T(8,128)(2,1)S(1)} %copy-done.4, bf16[256,336]{1,0:T(8,128)(2,1)S(1)} %copy-done.2), custom_call_target="tpu_custom_call" | custom-call | flops 301989888 | bytes 2097152 | tf_op jit(solution)/shard_map/pallas_call | solution.py:413
  34.6 0.6 %slice.7 = f32[1,4]{1,0:T(1,128)} slice(f32[8,128]{1,0:T(8,128)S(1)} %shard_map.68), slice={[2:3:1], [0:32:8]} | slice | bytes 32 | tf_op jit(solution)/shard_map/slice | solution.py:444
  35.2 0.1 reshape.7
  35.3 0.6 %copy.7 = f32[4,2,1,8]{3,2,1,0:T(1,128)} copy(f32[4,2,1,8]{3,0,1,2:T(4,128)S(1)} %bitcast.2) | data formatting | bytes 512
  (1 shorter events, 0.0 us)
Async XLA Ops:
  0.6 1.6 %copy-start = (bf16[4096,256]{1,0:T(8,128)(2,1)S(1)}, bf16[4096,256]{1,0:T(8,128)(2,1)}, u32[]{:S(2)}) copy-start(bf16[4096,256]{1,0:T(8,128)(2,1)} %snap_ref.1) | copy-start | bytes 6291460
  2.2 1.2 %copy-start.1 = (bf16[4096,128]{1,0:T(8,128)(2,1)S(1)}, bf16[4096,128]{1,0:T(8,128)(2,1)}, u32[]{:S(2)}) copy-start(bf16[4096,128]{1,0:T(8,128)(2,1)} %tail_ref.1) | copy-start | bytes 3145732
  3.4 0.9 %copy-start.2 = (bf16[256,336]{1,0:T(8,128)(2,1)S(1)}, bf16[256,336]{1,0:T(8,128)(2,1)}, u32[]{:S(2)}) copy-start(bf16[256,336]{1,0:T(8,128)(2,1)} %constant.8.clone.combine_ref) | copy-start | bytes 516100
  4.4 0.9 %copy-start.3 = (bf16[144,256]{1,0:T(8,128)(2,1)S(1)}, bf16[144,256]{1,0:T(8,128)(2,1)}, u32[]{:S(2)}) copy-start(bf16[144,256]{1,0:T(8,128)(2,1)} %constant.6.clone.table_ref) | copy-start | bytes 221188
  5.3 0.7 %copy-start.4 = (bf16[96,128]{1,0:T(8,128)(2,1)S(1)}, bf16[96,128]{1,0:T(8,128)(2,1)}, u32[]{:S(2)}) copy-start(bf16[96,128]{1,0:T(8,128)(2,1)} %constant.7.clone.tail_table_ref) | copy-start | bytes 73732

commit v2 on v1

--- a/solution.py
+++ b/solution.py
@@ -211,12 +211,13 @@
     for step in range(POWER):
         if step % 2 == 0:
             u_re, u_im = to_lanes(v_re, v_im)
-            mean = lane_sum(u_re * u_re + u_im * u_im) / entries
+            size = jnp.sqrt(lane_sum(u_re * u_re + u_im * u_im) / entries + 1e-06)
+            v_re, v_im = u_re, u_im
         else:
             u_re, u_im = to_rows(v_re, v_im)
-            mean = row_sum(u_re * u_re + u_im * u_im) / entries
-        size = jnp.sqrt(mean + 1e-06)
-        v_re, v_im = u_re / size, u_im / size
+            u_re, u_im = u_re / size, u_im / size
+            size = jnp.sqrt(row_sum(u_re * u_re + u_im * u_im) / entries + 1e-06)
+            v_re, v_im = u_re / size, u_im / size
     u_re, u_im = to_lanes(v_re, v_im)
     here = lane % nb == row
     across_re = row_sum(jnp.where(here, v_re, 0.0))
@@ -226,9 +227,9 @@
 
 
 def kernel(
-    zs, ns, nf, nb, scale,
-    snap_ref, tail_ref, table_ref, tail_table_ref, combine_ref, out_ref,
-    x_buf, tail_buf, table, tail_table, combine,
+    zs, ns, nf, nb, scale, spans, inner,
+    snap_ref, tail_ref, const_ref, gram_ref, value_ref,
+    x_buf, tail_buf, const,
     send, send_ext, recv, recv_ext, z_part, z_recv, s_recv,
     x_sem, const_sem, send_sem, recv_sem, ext_send_sem, ext_recv_sem,
     z_send_sem, z_recv_sem, s_send_sem, s_recv_sem,
@@ -243,11 +244,18 @@
     peers[0] = my_z
     friends = {k: xor_index(my_s, k, ns) for k in range(1, ns)}
 
+    barrier = pltpu.get_barrier_semaphore()
+    for k in order:
+        pl.semaphore_signal(barrier, inc=1, device_id=(my_s, peers[k]), device_id_type=MESH)
+    for k in range(1, ns):
+        pl.semaphore_signal(barrier, inc=1, device_id=(friends[k], my_z), device_id_type=MESH)
+
     loads = {}
+    (t0, t1), (l0, l1), (c0, c1) = spans
     constants = [
-        pltpu.make_async_copy(table_ref, table, const_sem.at[0]),
-        pltpu.make_async_copy(tail_table_ref, tail_table, const_sem.at[1]),
-        pltpu.make_async_copy(combine_ref, combine, const_sem.at[2]),
+        pltpu.make_async_copy(const_ref.at[a:b], const.at[a:b], const_sem.at[i])
+        for i, (a, b) in enumerate(spans)
+    ] + [
         pltpu.make_async_copy(
             tail_ref.at[pl.ds(pl.multiple_of(my_z * quarter, quarter), quarter)],
             tail_buf, const_sem.at[3],
@@ -264,17 +272,11 @@
     for copy in constants[1:]:
         copy.start()
 
-    barrier = pltpu.get_barrier_semaphore()
-    for k in order:
-        pl.semaphore_signal(barrier, inc=1, device_id=(my_s, peers[k]), device_id_type=MESH)
-    for k in range(1, ns):
-        pl.semaphore_signal(barrier, inc=1, device_id=(friends[k], my_z), device_id_type=MESH)
-
     ext_row = lax.broadcasted_iota(jnp.int32, (2 * pieces, LANES), 0) // 2
 
     def transform(k, s):
         loads[k, s].wait()
-        both = nt_dot(table[...], x_buf[k, s])
+        both = nt_dot(const[t0:t1, : x_buf.shape[3]], x_buf[k, s])
         rows = both.shape[0] // 2
         both = both[:rows] + both[rows:]
         extra = jnp.zeros((2 * pieces, LANES), jnp.float32)
@@ -317,7 +319,7 @@
 
     gram = jnp.zeros((width * nb, width * nb), jnp.float32)
     for s in range(SUBS):
-        last = nt_dot(tail_table[...], tail_buf[s * sub : (s + 1) * sub])
+        last = nt_dot(const[l0:l1, : tail_buf.shape[1]], tail_buf[s * sub : (s + 1) * sub])
         rows = last.shape[0] // 2
         last = (last[:rows] + last[rows:]).astype(jnp.bfloat16)
         for k in order:
@@ -334,7 +336,7 @@
             + [jnp.concatenate(extras, 0).astype(jnp.bfloat16), last],
             0,
         )
-        coef = jnp.dot(combine[...], stacked, preferred_element_type=jnp.float32)
+        coef = jnp.dot(const[c0:c1, :inner], stacked, preferred_element_type=jnp.float32)
         coef = coef.astype(jnp.bfloat16)
         gram = gram + nt_dot(coef, coef)
 
@@ -383,12 +385,19 @@
     mine = row == my_s
     row_re = jnp.sum(jnp.where(mine, g_re, 0.0), axis=0, keepdims=True)
     row_im = jnp.sum(jnp.where(mine, g_im, 0.0), axis=0, keepdims=True)
-    result = jnp.where(row == 0, row_re, jnp.where(row == 1, row_im, value))
     group = FREQ_DEV * nb
-    placed = result
+    result = jnp.where(row % 2 == 0, row_re, row_im)
+    placed, spread = result, value
     for z in range(1, zs):
         placed = jnp.where(my_z == z, pltpu.roll(result, LANES - z * group, 1), placed)
-    out_ref[...] = placed
+        spread = jnp.where(my_z == z, pltpu.roll(value, LANES - z * group, 1), spread)
+    rows, values = placed, spread
+    lane = lax.broadcasted_iota(jnp.int32, (nb, side), 1)
+    for f in range(1, FREQ_DEV):
+        rows = jnp.where(row // 2 == f, pltpu.roll(placed, LANES - f * nb, 1), rows)
+        values = jnp.where(lane == f, pltpu.roll(spread, LANES - f * (nb - 1), 1), values)
+    gram_ref[...] = rows
+    value_ref[...] = values
 
     for group_copies in copies.values():
         for copy in group_copies:
@@ -408,19 +417,23 @@
     combine = make_combine(nf, nb, pieces)
     window = 0.5 - 0.5 * np.cos(2.0 * np.pi * np.arange(NFFT) / NFFT)
     scale = float(1.0 / (points * ns * np.sum(window * window)))
+    parts = [table, tail_table, combine]
+    inner = combine.shape[1]
+    padded = -(-inner // LANES) * LANES
+    const = np.concatenate([np.pad(p, ((0, 0), (0, padded - p.shape[1]))) for p in parts], 0)
+    ends = np.cumsum([p.shape[0] for p in parts]).tolist()
+    spans = list(zip([0] + ends[:-1], ends))
     dma = pltpu.SemaphoreType.DMA
     flops = 2 * points * steps * table.shape[0]
-    packed = pl.pallas_call(
-        functools.partial(kernel, zs, ns, nf, nb, scale),
-        out_shape=jax.ShapeDtypeStruct((nb, LANES), jnp.float32),
-        in_specs=[pl.BlockSpec(memory_space=pl.ANY)] * 5,
-        out_specs=pl.BlockSpec(memory_space=pltpu.VMEM),
+    gram, values = pl.pallas_call(
+        functools.partial(kernel, zs, ns, nf, nb, scale, spans, inner),
+        out_shape=[jax.ShapeDtypeStruct((nb, LANES), jnp.float32)] * 2,
+        in_specs=[pl.BlockSpec(memory_space=pltpu.HBM)] * 3,
+        out_specs=[pl.BlockSpec(memory_space=pltpu.VMEM)] * 2,
         scratch_shapes=[
             pltpu.VMEM((zs, SUBS, sub, steps), jnp.bfloat16),
             pltpu.VMEM((points // zs, tail.shape[1]), jnp.bfloat16),
-            pltpu.VMEM(table.shape, jnp.bfloat16),
-            pltpu.VMEM(tail_table.shape, jnp.bfloat16),
-            pltpu.VMEM(combine.shape, jnp.bfloat16),
+            pltpu.VMEM(const.shape, jnp.bfloat16),
             pltpu.VMEM((zs, SUBS, 2 * width, sub), jnp.bfloat16),
             pltpu.VMEM((zs, SUBS, 2 * pieces, LANES), jnp.float32),
             pltpu.VMEM((zs, SUBS, 2 * width, sub), jnp.bfloat16),
@@ -433,15 +446,13 @@
             dma((zs,)), dma((zs,)), dma((ns,)), dma((ns,)),
         ],
         compiler_params=pltpu.CompilerParams(
-            collective_id=0, has_side_effects=True, vmem_limit_bytes=32 * 1024 * 1024
+            collective_id=0, has_side_effects=True, vmem_limit_bytes=56 * 1024 * 1024
         ),
         cost_estimate=pl.CostEstimate(
             flops=flops, bytes_accessed=points * steps * 2, transcendentals=0
         ),
-    )(snapshots, tail, jnp.asarray(table), jnp.asarray(tail_table), jnp.asarray(combine))
-    group = FREQ_DEV * nb
-    rows = packed[:2, :group].reshape(2, FREQ_DEV, 1, nb).transpose(1, 0, 2, 3)
-    return rows, packed[2, :group:nb]
+    )(snapshots, tail, jnp.asarray(const))
+    return gram[:, :nb].reshape(FREQ_DEV, 2, 1, nb), values[0, :FREQ_DEV]
 
 
 def power_of_two(count):

time: 36.2 us -> 31.7 us (0.88)
  local copies, waits for them, and re-layouts: 6.64 us -> 2.45 us
    unnamed x11 -> x1, local copies, waits for them, and re-layouts: 5.96 us -> 1.26 us
    squeeze x0 -> x1, local copies, waits for them, and re-layouts: none -> 1.18 us  [shards_kernel(): return (gram[:, :nb].reshape(FREQ_DEV, 2, 1, nb), values[0, :FREQ_DEV])]
    slice x2 -> x0, local copies, waits for them, and re-layouts: 0.6 us -> none  [the longest x1 0.59 us: shards_kernel(): return (rows, packed[2, :group:nb])]
where the time goes in v2:
time: 31.7 us; the launch traced here: 31.5 us
  Pallas kernels  28.4 us (90%)
  local copies, waits for them, and re-layouts  2.45 us (8%)
  between operations  0.64 us (2%)
    pallas_call x1, Pallas kernels, shards_kernel(): pl.pallas_call(functools.partial(kernel, zs, ns, nf, nb, scale, spans, in...  28.4 us
    unnamed x1, local copies, waits for them, and re-layouts  1.26 us
    squeeze x1, local copies, waits for them, and re-layouts, shards_kernel(): return (gram[:, :nb].reshape(FREQ_DEV, 2, 1, nb), values[0, :FREQ_DEV])  1.18 us

profile of v2, /device:TPU:0, one launch (start us, length us, event | category | flops | bytes accessed | tf_op | source)
XLA Modules:
  0.0 31.5 jit_solution(16425145004680068654)
XLA Ops:
  0.6 28.4 %shard_map.50 = (f32[8,128]{1,0:T(8,128)}, f32[8,128]{1,0:T(8,128)}) custom-call(bf16[4096,256]{1,0:T(8,128)(2,1)} %snap_ref.1, bf16[4096,128]{1,0:T(8,128)(2,1)} %tail_ref.1, bf16[496,384]{1,0:T(8,128)(2,1)} %constant.2.clone.const_ref), custom_call_target="tpu_custom_call" | custom-call | flops 301989888 | bytes 2097152 | tf_op jit(solution)/shard_map/pallas_call | solution.py:428
  29.1 1.2 %slice_bitcast_fusion = f32[4]{0:T(128)} fusion(f32[8,128]{1,0:T(8,128)} %get-tuple-element.5), kind=kLoop, calls=%fused_computation | loop fusion | bytes 32 | tf_op jit(solution)/shard_map/squeeze | solution.py:455
  30.2 1.3 %copy.7 = f32[4,2,1,8]{3,2,1,0:T(1,128)} copy(f32[4,2,1,8]{3,2,1,0:T(1,128)} %bitcast.6) | data formatting | bytes 512

commit v3 on v2

--- a/solution.py
+++ b/solution.py
@@ -14,7 +14,7 @@
 NFFT = 256
 POWER = 4
 LANES = 128
-SUBS = 2
+SUBS = 4
 MESH = pl.DeviceIdType.MESH
 
 
@@ -124,10 +124,10 @@
     main, extra = half_rows(nf)
     half = NFFT // 2
     width = 2 * nf
-    both = np.zeros((2 * width + 2 * pieces, NFFT))
+    both = np.zeros((2 * width + max(2 * pieces, 8), NFFT))
     for h in range(2):
         both[h * width : (h + 1) * width, h * half : (h + 1) * half] = main
-        both[2 * width + h :: 2, h * half : (h + 1) * half] = extra
+        both[2 * width + h : 2 * width + 2 * pieces : 2, h * half : (h + 1) * half] = extra
     last = np.zeros((width + 16, half))
     last[:width] = main
     last[width] = extra[0]
@@ -229,7 +229,7 @@
 def kernel(
     zs, ns, nf, nb, scale, spans, inner,
     snap_ref, tail_ref, const_ref, gram_ref, value_ref,
-    x_buf, tail_buf, const,
+    x_buf, tail_buf, last_buf, const,
     send, send_ext, recv, recv_ext, z_part, z_recv, s_recv,
     x_sem, const_sem, send_sem, recv_sem, ext_send_sem, ext_recv_sem,
     z_send_sem, z_recv_sem, s_send_sem, s_recv_sem,
@@ -282,7 +282,7 @@
         extra = jnp.zeros((2 * pieces, LANES), jnp.float32)
         for q in range(pieces):
             extra = jnp.where(
-                ext_row == q, both[2 * width :, q * LANES : (q + 1) * LANES], extra
+                ext_row == q, both[2 * width : 2 * width + 2 * pieces, q * LANES : (q + 1) * LANES], extra
             )
         return both[: 2 * width].astype(jnp.bfloat16), extra
 
@@ -316,12 +316,13 @@
         recv_ext[my_z, s] = extra
     for copy in constants[1:]:
         copy.wait()
-
-    gram = jnp.zeros((width * nb, width * nb), jnp.float32)
     for s in range(SUBS):
         last = nt_dot(const[l0:l1, : tail_buf.shape[1]], tail_buf[s * sub : (s + 1) * sub])
         rows = last.shape[0] // 2
-        last = (last[:rows] + last[rows:]).astype(jnp.bfloat16)
+        last_buf[s] = (last[:rows] + last[rows:]).astype(jnp.bfloat16)
+
+    gram = jnp.zeros((width * nb, width * nb), jnp.float32)
+    for s in range(SUBS):
         for k in order:
             for copy in copies[k, s]:
                 copy.wait_recv()
@@ -333,7 +334,7 @@
             )
         stacked = jnp.concatenate(
             [recv[d, s] for d in range(zs)]
-            + [jnp.concatenate(extras, 0).astype(jnp.bfloat16), last],
+            + [jnp.concatenate(extras, 0).astype(jnp.bfloat16), last_buf[s]],
             0,
         )
         coef = jnp.dot(const[c0:c1, :inner], stacked, preferred_element_type=jnp.float32)
@@ -433,6 +434,7 @@
         scratch_shapes=[
             pltpu.VMEM((zs, SUBS, sub, steps), jnp.bfloat16),
             pltpu.VMEM((points // zs, tail.shape[1]), jnp.bfloat16),
+            pltpu.VMEM((SUBS, tail_table.shape[0] // 2, sub), jnp.bfloat16),
             pltpu.VMEM(const.shape, jnp.bfloat16),
             pltpu.VMEM((zs, SUBS, 2 * width, sub), jnp.bfloat16),
             pltpu.VMEM((zs, SUBS, 2 * pieces, LANES), jnp.float32),
@@ -446,7 +448,7 @@
             dma((zs,)), dma((zs,)), dma((ns,)), dma((ns,)),
         ],
         compiler_params=pltpu.CompilerParams(
-            collective_id=0, has_side_effects=True, vmem_limit_bytes=56 * 1024 * 1024
+            collective_id=0, has_side_effects=True, vmem_limit_bytes=55040 * 1024
         ),
         cost_estimate=pl.CostEstimate(
             flops=flops, bytes_accessed=points * steps * 2, transcendentals=0
@@ -464,7 +466,7 @@
     points, steps = snapshots.shape
     nb = zs * steps // (NFFT // 2)
     packs = FREQ_DEV * zs * nb == LANES and steps == NFFT and nb == ns == 8
-    whole = points % (zs * SUBS * LANES * 4) == 0
+    whole = points % (zs * SUBS * LANES) == 0
     if packs and whole and power_of_two(zs) and power_of_two(ns):
         return shards_kernel(zs, ns, snapshots, tail)
     return shards_general(snapshots, tail)

time: 31.7 us -> 30.2 us (0.953)
  local copies, waits for them, and re-layouts: 2.45 us -> 1.11 us
    unnamed x1, local copies, waits for them, and re-layouts: 1.26 us -> 0.59 us
    squeeze x1, local copies, waits for them, and re-layouts: 1.18 us -> 0.51 us  [shards_kernel(): return (gram[:, :nb].reshape(FREQ_DEV, 2, 1, nb), values[0, :FREQ_DEV])]
where the time goes in v3:
time: 30.2 us; the launch traced here: 30.1 us
  Pallas kernels  28.4 us (94%)
  local copies, waits for them, and re-layouts  1.11 us (4%)
  between operations  0.64 us (2%)
    pallas_call x1, Pallas kernels, shards_kernel(): pl.pallas_call(functools.partial(kernel, zs, ns, nf, nb, scale, spans, in...  28.4 us

profile of v3, /device:TPU:0, one launch (start us, length us, event | category | flops | bytes accessed | tf_op | source)
XLA Modules:
  0.0 30.1 jit_solution(16940965732453694578)
XLA Ops:
  0.6 28.4 %shard_map.50 = (f32[8,128]{1,0:T(8,128)S(1)}, f32[8,128]{1,0:T(8,128)S(1)}) custom-call(bf16[4096,256]{1,0:T(8,128)(2,1)} %snap_ref.1, bf16[4096,128]{1,0:T(8,128)(2,1)} %tail_ref.1, bf16[496,384]{1,0:T(8,128)(2,1)} %constant.2.clone.const_ref), custom_call_target="tpu_custom_call" | custom-call | flops 301989888 | bytes 2097152 | tf_op jit(solution)/shard_map/pallas_call | solution.py:429
  29.0 0.5 %slice_bitcast_fusion = f32[4]{0:T(128)} fusion(f32[8,128]{1,0:T(8,128)S(1)} %get-tuple-element.5), kind=kLoop, calls=%fused_computation | loop fusion | bytes 32 | tf_op jit(solution)/shard_map/squeeze | solution.py:457
  29.5 0.6 %copy.7 = f32[4,2,1,8]{3,2,1,0:T(1,128)} copy(f32[4,2,1,8]{3,2,1,0:T(1,128)S(1)} %bitcast.6) | data formatting | bytes 512

commit v4 on v3

--- a/solution.py
+++ b/solution.py
@@ -211,13 +211,13 @@
     for step in range(POWER):
         if step % 2 == 0:
             u_re, u_im = to_lanes(v_re, v_im)
-            size = jnp.sqrt(lane_sum(u_re * u_re + u_im * u_im) / entries + 1e-06)
+            scale = lax.rsqrt(lane_sum(u_re * u_re + u_im * u_im) / entries + 1e-06)
             v_re, v_im = u_re, u_im
         else:
             u_re, u_im = to_rows(v_re, v_im)
-            u_re, u_im = u_re / size, u_im / size
-            size = jnp.sqrt(row_sum(u_re * u_re + u_im * u_im) / entries + 1e-06)
-            v_re, v_im = u_re / size, u_im / size
+            u_re, u_im = u_re * scale, u_im * scale
+            scale = lax.rsqrt(row_sum(u_re * u_re + u_im * u_im) / entries + 1e-06)
+            v_re, v_im = u_re * scale, u_im * scale
     u_re, u_im = to_lanes(v_re, v_im)
     here = lane % nb == row
     across_re = row_sum(jnp.where(here, v_re, 0.0))
@@ -239,9 +239,17 @@
     sub = quarter // SUBS
     width = 2 * nf
     pieces = sub // LANES
-    order = list(range(zs // 2, zs)) + list(range(1, zs // 2))
-    peers = {k: xor_index(my_z, k, zs) for k in order}
-    peers[0] = my_z
+    far = list(range(zs // 2, zs))
+    near = list(range(1, zs // 2))
+    beside = lax.rem((my_z + zs // 4) // (zs // 2), 2)
+    order = list(range(1, zs))
+    steps = {0: 0}
+    peers = {0: my_z}
+    for i, (inner_k, outer_k) in enumerate(zip(near + far, far + near), 1):
+        steps[i] = beside * inner_k + (1 - beside) * outer_k
+        peers[i] = beside * xor_index(my_z, inner_k, zs) + (1 - beside) * xor_index(
+            my_z, outer_k, zs
+        )
     friends = {k: xor_index(my_s, k, ns) for k in range(1, ns)}
 
     barrier = pltpu.get_barrier_semaphore()
@@ -299,12 +307,12 @@
             copies[k, s] = [
                 pltpu.make_async_remote_copy(
                     send_ext.at[k, s], recv_ext.at[my_z, s],
-                    ext_send_sem.at[k, s], ext_recv_sem.at[k, s],
+                    ext_send_sem.at[k, s], ext_recv_sem.at[steps[k], s],
                     device_id=target, device_id_type=MESH,
                 ),
                 pltpu.make_async_remote_copy(
                     send.at[k, s], recv.at[my_z, s],
-                    send_sem.at[k, s], recv_sem.at[k, s],
+                    send_sem.at[k, s], recv_sem.at[steps[k], s],
                     device_id=target, device_id_type=MESH,
                 ),
             ]
@@ -356,14 +364,15 @@
     z_copies = []
     for k in order:
         copy = pltpu.make_async_remote_copy(
-            z_part, z_recv.at[k], z_send_sem.at[k], z_recv_sem.at[k],
+            z_part, z_recv.at[steps[k]], z_send_sem.at[k], z_recv_sem.at[steps[k]],
             device_id=(my_s, peers[k]), device_id_type=MESH,
         )
         copy.start()
         z_copies.append(copy)
+    for copy in z_copies:
+        copy.wait_recv()
     total = z_part[...]
-    for k, copy in zip(order, z_copies):
-        copy.wait_recv()
+    for k in order:
         total = total + z_recv[k]
     s_recv[my_s] = total
     s_copies = []

time: 30.2 us -> 30.5 us (level)
  no operation moved by 1% of the time
where the time goes in v4:
time: 30.5 us; the launch traced here: 30.3 us
  Pallas kernels  28.6 us (94%)
  local copies, waits for them, and re-layouts  1.11 us (4%)
  between operations  0.64 us (2%)
    pallas_call x1, Pallas kernels, shards_kernel(): pl.pallas_call(functools.partial(kernel, zs, ns, nf, nb, scale, spans, in...  28.6 us

profile of v4, /device:TPU:0, one launch (start us, length us, event | category | flops | bytes accessed | tf_op | source)
XLA Modules:
  0.0 30.3 jit_solution(17183604685574960436)
XLA Ops:
  0.6 28.6 %shard_map.50 = (f32[8,128]{1,0:T(8,128)S(1)}, f32[8,128]{1,0:T(8,128)S(1)}) custom-call(bf16[4096,256]{1,0:T(8,128)(2,1)} %snap_ref.1, bf16[4096,128]{1,0:T(8,128)(2,1)} %tail_ref.1, bf16[496,384]{1,0:T(8,128)(2,1)} %constant.2.clone.const_ref), custom_call_target="tpu_custom_call" | custom-call | flops 301989888 | bytes 2097152 | tf_op jit(solution)/shard_map/pallas_call | solution.py:438
  29.2 0.5 %slice_bitcast_fusion = f32[4]{0:T(128)} fusion(f32[8,128]{1,0:T(8,128)S(1)} %get-tuple-element.5), kind=kLoop, calls=%fused_computation | loop fusion | bytes 32 | tf_op jit(solution)/shard_map/squeeze | solution.py:466
  29.7 0.6 %copy.7 = f32[4,2,1,8]{3,2,1,0:T(1,128)} copy(f32[4,2,1,8]{3,2,1,0:T(1,128)S(1)} %bitcast.6) | data formatting | bytes 512

commit v5 on v3

--- a/solution.py
+++ b/solution.py
@@ -171,8 +171,8 @@
     result = 0
     bit = 1
     while bit < count:
-        digit = lax.rem(index // bit, 2)
-        result = result + bit * ((1 - digit) if other & bit else digit)
+        left, right = lax.rem(index // bit, 2), lax.rem(other // bit, 2)
+        result = result + bit * (left + right - 2 * left * right)
         bit *= 2
     return result
 
@@ -211,13 +211,13 @@
     for step in range(POWER):
         if step % 2 == 0:
             u_re, u_im = to_lanes(v_re, v_im)
-            size = jnp.sqrt(lane_sum(u_re * u_re + u_im * u_im) / entries + 1e-06)
+            scale = lax.rsqrt(lane_sum(u_re * u_re + u_im * u_im) / entries + 1e-06)
             v_re, v_im = u_re, u_im
         else:
             u_re, u_im = to_rows(v_re, v_im)
-            u_re, u_im = u_re / size, u_im / size
-            size = jnp.sqrt(row_sum(u_re * u_re + u_im * u_im) / entries + 1e-06)
-            v_re, v_im = u_re / size, u_im / size
+            u_re, u_im = u_re * scale, u_im * scale
+            scale = lax.rsqrt(row_sum(u_re * u_re + u_im * u_im) / entries + 1e-06)
+            v_re, v_im = u_re * scale, u_im * scale
     u_re, u_im = to_lanes(v_re, v_im)
     here = lane % nb == row
     across_re = row_sum(jnp.where(here, v_re, 0.0))
@@ -229,7 +229,7 @@
 def kernel(
     zs, ns, nf, nb, scale, spans, inner,
     snap_ref, tail_ref, const_ref, gram_ref, value_ref,
-    x_buf, tail_buf, last_buf, const,
+    x_buf, tail_buf, last_buf, gram_buf, const,
     send, send_ext, recv, recv_ext, z_part, z_recv, s_recv,
     x_sem, const_sem, send_sem, recv_sem, ext_send_sem, ext_recv_sem,
     z_send_sem, z_recv_sem, s_send_sem, s_recv_sem,
@@ -239,18 +239,26 @@
     sub = quarter // SUBS
     width = 2 * nf
     pieces = sub // LANES
-    order = list(range(zs // 2, zs)) + list(range(1, zs // 2))
-    peers = {k: xor_index(my_z, k, zs) for k in order}
-    peers[0] = my_z
-    friends = {k: xor_index(my_s, k, ns) for k in range(1, ns)}
+
+    def peer(k):
+        return xor_index(my_z, k, zs)
+
+    def friend(k):
+        return xor_index(my_s, k, ns)
 
     barrier = pltpu.get_barrier_semaphore()
-    for k in order:
-        pl.semaphore_signal(barrier, inc=1, device_id=(my_s, peers[k]), device_id_type=MESH)
-    for k in range(1, ns):
-        pl.semaphore_signal(barrier, inc=1, device_id=(friends[k], my_z), device_id_type=MESH)
-
-    loads = {}
+
+    def greet_peer(k, carry):
+        pl.semaphore_signal(barrier, inc=1, device_id=(my_s, peer(k)), device_id_type=MESH)
+        return carry
+
+    def greet_friend(k, carry):
+        pl.semaphore_signal(barrier, inc=1, device_id=(friend(k), my_z), device_id_type=MESH)
+        return carry
+
+    lax.fori_loop(1, zs, greet_peer, 0)
+    lax.fori_loop(1, ns, greet_friend, 0)
+
     (t0, t1), (l0, l1), (c0, c1) = spans
     constants = [
         pltpu.make_async_copy(const_ref.at[a:b], const.at[a:b], const_sem.at[i])
@@ -261,70 +269,91 @@
             tail_buf, const_sem.at[3],
         ),
     ]
+
+    def place(t):
+        return lax.rem(t + zs // 2, zs), t // zs
+
+    def load(t):
+        k, s = place(t)
+        first = pl.multiple_of(peer(k) * quarter + s * sub, sub)
+        return pltpu.make_async_copy(
+            snap_ref.at[pl.ds(first, sub)], x_buf.at[k, s], x_sem.at[k, s]
+        )
+
+    def send_copies(k, s):
+        target = (my_s, peer(k))
+        return [
+            pltpu.make_async_remote_copy(
+                send_ext.at[k, s], recv_ext.at[my_z, s],
+                ext_send_sem.at[k, s], ext_recv_sem.at[k, s],
+                device_id=target, device_id_type=MESH,
+            ),
+            pltpu.make_async_remote_copy(
+                send.at[k, s], recv.at[my_z, s],
+                send_sem.at[k, s], recv_sem.at[k, s],
+                device_id=target, device_id_type=MESH,
+            ),
+        ]
+
+    def start_load(t, carry):
+        load(t).start()
+        return carry
+
     constants[0].start()
-    for s in range(SUBS):
-        for k in order + [0]:
-            first = pl.multiple_of(peers[k] * quarter + s * sub, sub)
-            loads[k, s] = pltpu.make_async_copy(
-                snap_ref.at[pl.ds(first, sub)], x_buf.at[k, s], x_sem.at[k, s]
-            )
-            loads[k, s].start()
+    lax.fori_loop(0, zs * SUBS, start_load, 0)
     for copy in constants[1:]:
         copy.start()
-
     ext_row = lax.broadcasted_iota(jnp.int32, (2 * pieces, LANES), 0) // 2
-
-    def transform(k, s):
-        loads[k, s].wait()
+    constants[0].wait()
+    pl.semaphore_wait(barrier, zs - 1 + ns - 1)
+
+    def transform(t, carry):
+        k, s = place(t)
+        load(t).wait()
         both = nt_dot(const[t0:t1, : x_buf.shape[3]], x_buf[k, s])
         rows = both.shape[0] // 2
         both = both[:rows] + both[rows:]
         extra = jnp.zeros((2 * pieces, LANES), jnp.float32)
         for q in range(pieces):
             extra = jnp.where(
-                ext_row == q, both[2 * width : 2 * width + 2 * pieces, q * LANES : (q + 1) * LANES], extra
+                ext_row == q,
+                both[2 * width : 2 * width + 2 * pieces, q * LANES : (q + 1) * LANES],
+                extra,
             )
-        return both[: 2 * width].astype(jnp.bfloat16), extra
-
-    constants[0].wait()
-    copies = {}
-    for s in range(SUBS):
-        for k in order:
-            main, extra = transform(k, s)
+        main = both[: 2 * width].astype(jnp.bfloat16)
+
+        @pl.when(k == 0)
+        def _():
+            recv[my_z, s] = main
+            recv_ext[my_z, s] = extra
+
+        @pl.when(k > 0)
+        def _():
             send[k, s] = main
             send_ext[k, s] = extra
-            if s == 0 and k == order[0]:
-                pl.semaphore_wait(barrier, zs - 1 + ns - 1)
-            target = (my_s, peers[k])
-            copies[k, s] = [
-                pltpu.make_async_remote_copy(
-                    send_ext.at[k, s], recv_ext.at[my_z, s],
-                    ext_send_sem.at[k, s], ext_recv_sem.at[k, s],
-                    device_id=target, device_id_type=MESH,
-                ),
-                pltpu.make_async_remote_copy(
-                    send.at[k, s], recv.at[my_z, s],
-                    send_sem.at[k, s], recv_sem.at[k, s],
-                    device_id=target, device_id_type=MESH,
-                ),
-            ]
-            for copy in copies[k, s]:
+            for copy in send_copies(k, s):
                 copy.start()
-    for s in range(SUBS):
-        main, extra = transform(0, s)
-        recv[my_z, s] = main
-        recv_ext[my_z, s] = extra
+
+        return carry
+
+    lax.fori_loop(0, zs * SUBS, transform, 0)
+
     for copy in constants[1:]:
         copy.wait()
-    for s in range(SUBS):
-        last = nt_dot(const[l0:l1, : tail_buf.shape[1]], tail_buf[s * sub : (s + 1) * sub])
+
+    def transform_tail(s, carry):
+        points = tail_buf[pl.ds(pl.multiple_of(s * sub, sub), sub)]
+        last = nt_dot(const[l0:l1, : tail_buf.shape[1]], points)
         rows = last.shape[0] // 2
         last_buf[s] = (last[:rows] + last[rows:]).astype(jnp.bfloat16)
-
-    gram = jnp.zeros((width * nb, width * nb), jnp.float32)
-    for s in range(SUBS):
-        for k in order:
-            for copy in copies[k, s]:
+        return carry
+
+    lax.fori_loop(0, SUBS, transform_tail, 0)
+    gram_buf[...] = jnp.zeros(gram_buf.shape, jnp.float32)
+
+    def combine(s, carry):
+        for k in range(1, zs):
+            for copy in send_copies(k, s):
                 copy.wait_recv()
         extras = []
         for d in range(zs):
@@ -339,11 +368,14 @@
         )
         coef = jnp.dot(const[c0:c1, :inner], stacked, preferred_element_type=jnp.float32)
         coef = coef.astype(jnp.bfloat16)
-        gram = gram + nt_dot(coef, coef)
+        gram_buf[...] += nt_dot(coef, coef)
+        return carry
+
+    lax.fori_loop(0, SUBS, combine, 0)
 
     side = nf * nb
-    real = gram[:side, :side] + gram[side:, side:]
-    imag = gram[:side, side:] - gram[side:, :side]
+    real = gram_buf[:side, :side] + gram_buf[side:, side:]
+    imag = gram_buf[:side, side:] - gram_buf[side:, :side]
     lane_freq = lax.broadcasted_iota(jnp.int32, (nb, side), 1) // nb
     g_re = jnp.zeros((nb, side), jnp.float32)
     g_im = jnp.zeros((nb, side), jnp.float32)
@@ -353,29 +385,33 @@
     z_part[0] = g_re * scale
     z_part[1] = g_im * scale
 
-    z_copies = []
-    for k in order:
-        copy = pltpu.make_async_remote_copy(
+    def z_copy(k):
+        return pltpu.make_async_remote_copy(
             z_part, z_recv.at[k], z_send_sem.at[k], z_recv_sem.at[k],
-            device_id=(my_s, peers[k]), device_id_type=MESH,
+            device_id=(my_s, peer(k)), device_id_type=MESH,
         )
-        copy.start()
-        z_copies.append(copy)
+
+    def s_copy(k):
+        return pltpu.make_async_remote_copy(
+            s_recv.at[my_s], s_recv.at[my_s], s_send_sem.at[k], s_recv_sem.at[k],
+            device_id=(friend(k), my_z), device_id_type=MESH,
+        )
+
+    def run(first, last, action):
+        def body(k, carry):
+            action(k)
+            return carry
+
+        lax.fori_loop(first, last, body, 0)
+
+    run(1, zs, lambda k: z_copy(k).start())
+    run(1, zs, lambda k: z_copy(k).wait_recv())
     total = z_part[...]
-    for k, copy in zip(order, z_copies):
-        copy.wait_recv()
+    for k in range(1, zs):
         total = total + z_recv[k]
     s_recv[my_s] = total
-    s_copies = []
-    for k in range(1, ns):
-        copy = pltpu.make_async_remote_copy(
-            s_recv.at[my_s], s_recv.at[my_s], s_send_sem.at[k], s_recv_sem.at[k],
-            device_id=(friends[k], my_z), device_id_type=MESH,
-        )
-        copy.start()
-        s_copies.append(copy)
-    for copy in s_copies:
-        copy.wait_recv()
+    run(1, ns, lambda k: s_copy(k).start())
+    run(1, ns, lambda k: s_copy(k).wait_recv())
     total = s_recv[0]
     for d in range(1, ns):
         total = total + s_recv[d]
@@ -400,11 +436,14 @@
     gram_ref[...] = rows
     value_ref[...] = values
 
-    for group_copies in copies.values():
-        for copy in group_copies:
-            copy.wait_send()
-    for copy in z_copies + s_copies:
-        copy.wait_send()
+    def finish(k):
+        for s in range(SUBS):
+            for copy in send_copies(k, s):
+                copy.wait_send()
+        z_copy(k).wait_send()
+
+    run(1, zs, finish)
+    run(1, ns, lambda k: s_copy(k).wait_send())
 
 
 def shards_kernel(zs, ns, snapshots, tail):
@@ -435,6 +474,7 @@
             pltpu.VMEM((zs, SUBS, sub, steps), jnp.bfloat16),
             pltpu.VMEM((points // zs, tail.shape[1]), jnp.bfloat16),
             pltpu.VMEM((SUBS, tail_table.shape[0] // 2, sub), jnp.bfloat16),
+            pltpu.VMEM((width * nb, width * nb), jnp.float32),
             pltpu.VMEM(const.shape, jnp.bfloat16),
             pltpu.VMEM((zs, SUBS, 2 * width, sub), jnp.bfloat16),
             pltpu.VMEM((zs, SUBS, 2 * pieces, LANES), jnp.float32),

time: 30.2 us -> 30.7 us (1.017)
  Pallas kernels: 28.4 us -> 28.9 us
    pallas_call x1, Pallas kernels: 28.4 us -> 28.9 us  [shards_kernel(): pl.pallas_call(functools.partial(kernel, zs, ns, nf, nb, scale, spans, in...]
where the time goes in v5:
time: 30.7 us; the launch traced here: 30.6 us
  Pallas kernels  28.9 us (94%)
  local copies, waits for them, and re-layouts  1.11 us (4%)
  between operations  0.64 us (2%)
    pallas_call x1, Pallas kernels, shards_kernel(): pl.pallas_call(functools.partial(kernel, zs, ns, nf, nb, scale, spans, in...  28.9 us

profile of v5, /device:TPU:0, one launch (start us, length us, event | category | flops | bytes accessed | tf_op | source)
XLA Modules:
  0.0 30.6 jit_solution(7268500963402908810)
XLA Ops:
  0.6 28.9 %shard_map.50 = (f32[8,128]{1,0:T(8,128)S(1)}, f32[8,128]{1,0:T(8,128)S(1)}) custom-call(bf16[4096,256]{1,0:T(8,128)(2,1)} %snap_ref.1, bf16[4096,128]{1,0:T(8,128)(2,1)} %tail_ref.1, bf16[496,384]{1,0:T(8,128)(2,1)} %constant.2.clone.const_ref), custom_call_target="tpu_custom_call" | custom-call | flops 301989888 | bytes 2097152 | tf_op jit(solution)/shard_map/pallas_call | solution.py:468
  29.5 0.5 %slice_bitcast_fusion = f32[4]{0:T(128)} fusion(f32[8,128]{1,0:T(8,128)S(1)} %get-tuple-element.5), kind=kLoop, calls=%fused_computation | loop fusion | bytes 32 | tf_op jit(solution)/shard_map/squeeze | solution.py:497
  30.0 0.6 %copy.7 = f32[4,2,1,8]{3,2,1,0:T(1,128)} copy(f32[4,2,1,8]{3,2,1,0:T(1,128)S(1)} %bitcast.6) | data formatting | bytes 512

commit v6 on v3

--- a/solution.py
+++ b/solution.py
@@ -124,14 +124,15 @@
     main, extra = half_rows(nf)
     half = NFFT // 2
     width = 2 * nf
-    both = np.zeros((2 * width + max(2 * pieces, 8), NFFT))
+    both = np.zeros((2 * width, NFFT))
+    extras = np.zeros((2 * pieces, NFFT))
     for h in range(2):
         both[h * width : (h + 1) * width, h * half : (h + 1) * half] = main
-        both[2 * width + h : 2 * width + 2 * pieces : 2, h * half : (h + 1) * half] = extra
+        extras[h::2, h * half : (h + 1) * half] = extra
     last = np.zeros((width + 16, half))
     last[:width] = main
     last[width] = extra[0]
-    return two_pieces(both), two_pieces(last)
+    return two_pieces(both), two_pieces(extras), two_pieces(last)
 
 
 def make_combine(nf, nb, pieces):
@@ -211,13 +212,13 @@
     for step in range(POWER):
         if step % 2 == 0:
             u_re, u_im = to_lanes(v_re, v_im)
-            size = jnp.sqrt(lane_sum(u_re * u_re + u_im * u_im) / entries + 1e-06)
+            scale = lax.rsqrt(lane_sum(u_re * u_re + u_im * u_im) / entries + 1e-06)
             v_re, v_im = u_re, u_im
         else:
             u_re, u_im = to_rows(v_re, v_im)
-            u_re, u_im = u_re / size, u_im / size
-            size = jnp.sqrt(row_sum(u_re * u_re + u_im * u_im) / entries + 1e-06)
-            v_re, v_im = u_re / size, u_im / size
+            u_re, u_im = u_re * scale, u_im * scale
+            scale = lax.rsqrt(row_sum(u_re * u_re + u_im * u_im) / entries + 1e-06)
+            v_re, v_im = u_re * scale, u_im * scale
     u_re, u_im = to_lanes(v_re, v_im)
     here = lane % nb == row
     across_re = row_sum(jnp.where(here, v_re, 0.0))
@@ -238,7 +239,8 @@
     quarter = snap_ref.shape[0] // zs
     sub = quarter // SUBS
     width = 2 * nf
-    pieces = sub // LANES
+    pieces = quarter // LANES
+    here = sub // LANES
     order = list(range(zs // 2, zs)) + list(range(1, zs // 2))
     peers = {k: xor_index(my_z, k, zs) for k in order}
     peers[0] = my_z
@@ -251,10 +253,10 @@
         pl.semaphore_signal(barrier, inc=1, device_id=(friends[k], my_z), device_id_type=MESH)
 
     loads = {}
-    (t0, t1), (l0, l1), (c0, c1) = spans
+    (t0, _), (e0, e1), (l0, l1), (c0, c1) = spans
     constants = [
         pltpu.make_async_copy(const_ref.at[a:b], const.at[a:b], const_sem.at[i])
-        for i, (a, b) in enumerate(spans)
+        for i, (a, b) in enumerate([(t0, e1), (l0, l1), (c0, c1)])
     ] + [
         pltpu.make_async_copy(
             tail_ref.at[pl.ds(pl.multiple_of(my_z * quarter, quarter), quarter)],
@@ -268,52 +270,66 @@
             loads[k, s] = pltpu.make_async_copy(
                 snap_ref.at[pl.ds(first, sub)], x_buf.at[k, s], x_sem.at[k, s]
             )
-            loads[k, s].start()
-    for copy in constants[1:]:
-        copy.start()
+    for k in order:
+        loads[k, 0].start()
 
     ext_row = lax.broadcasted_iota(jnp.int32, (2 * pieces, LANES), 0) // 2
 
+    def folded(x):
+        rows = x.shape[0] // 2
+        return x[:rows] + x[rows:]
+
     def transform(k, s):
-        loads[k, s].wait()
-        both = nt_dot(const[t0:t1, : x_buf.shape[3]], x_buf[k, s])
-        rows = both.shape[0] // 2
-        both = both[:rows] + both[rows:]
+        return folded(nt_dot(const[t0:e0, : x_buf.shape[3]], x_buf[k, s])).astype(jnp.bfloat16)
+
+    def extras_of(k):
+        whole = x_buf[k].reshape(quarter, x_buf.shape[3])
+        rows = folded(nt_dot(const[e0:e1, : x_buf.shape[3]], whole))
         extra = jnp.zeros((2 * pieces, LANES), jnp.float32)
         for q in range(pieces):
-            extra = jnp.where(
-                ext_row == q, both[2 * width : 2 * width + 2 * pieces, q * LANES : (q + 1) * LANES], extra
-            )
-        return both[: 2 * width].astype(jnp.bfloat16), extra
+            extra = jnp.where(ext_row == q, rows[:, q * LANES : (q + 1) * LANES], extra)
+        return extra.astype(jnp.bfloat16)
+
+    def started(source, target, send_sems, recv_sems, k):
+        copy = pltpu.make_async_remote_copy(
+            source, target, send_sems, recv_sems,
+            device_id=(my_s, peers[k]), device_id_type=MESH,
+        )
+        copy.start()
+        return copy
 
     constants[0].wait()
     copies = {}
     for s in range(SUBS):
         for k in order:
-            main, extra = transform(k, s)
-            send[k, s] = main
-            send_ext[k, s] = extra
+            if s < 2:
+                loads[k, s].wait()
+            send[k, s] = transform(k, s)
             if s == 0 and k == order[0]:
                 pl.semaphore_wait(barrier, zs - 1 + ns - 1)
-            target = (my_s, peers[k])
-            copies[k, s] = [
-                pltpu.make_async_remote_copy(
-                    send_ext.at[k, s], recv_ext.at[my_z, s],
-                    ext_send_sem.at[k, s], ext_recv_sem.at[k, s],
-                    device_id=target, device_id_type=MESH,
-                ),
-                pltpu.make_async_remote_copy(
-                    send.at[k, s], recv.at[my_z, s],
-                    send_sem.at[k, s], recv_sem.at[k, s],
-                    device_id=target, device_id_type=MESH,
-                ),
-            ]
-            for copy in copies[k, s]:
-                copy.start()
+            copies[k, s] = started(
+                send.at[k, s], recv.at[my_z, s], send_sem.at[k, s], recv_sem.at[k, s], k
+            )
+            if s == 0 and k == order[0]:
+                for later in range(1, SUBS):
+                    for i in order:
+                        loads[i, later].start()
+                for i in range(SUBS):
+                    loads[0, i].start()
+                for copy in constants[1:]:
+                    copy.start()
+        if s == 1:
+            for k in order:
+                for later in range(2, SUBS):
+                    loads[k, later].wait()
+                send_ext[k] = extras_of(k)
+                copies[k, "ext"] = started(
+                    send_ext.at[k], recv_ext.at[my_z], ext_send_sem.at[k], ext_recv_sem.at[k], k
+                )
     for s in range(SUBS):
-        main, extra = transform(0, s)
-        recv[my_z, s] = main
-        recv_ext[my_z, s] = extra
+        loads[0, s].wait()
+        recv[my_z, s] = transform(0, s)
+    recv_ext[my_z] = extras_of(0)
     for copy in constants[1:]:
         copy.wait()
     for s in range(SUBS):
@@ -324,17 +340,24 @@
     gram = jnp.zeros((width * nb, width * nb), jnp.float32)
     for s in range(SUBS):
         for k in order:
-            for copy in copies[k, s]:
-                copy.wait_recv()
+            copies[k, s].wait_recv()
+            if s == 0:
+                copies[k, "ext"].wait_recv()
         extras = []
         for d in range(zs):
-            extra = recv_ext[d, s]
+            extra = recv_ext[d]
             extras.append(
-                jnp.concatenate([jnp.where(ext_row == q, extra, 0.0) for q in range(pieces)], 1)
+                jnp.concatenate(
+                    [
+                        jnp.where(ext_row == s * here + q, extra, jnp.zeros_like(extra))
+                        for q in range(here)
+                    ],
+                    1,
+                )
             )
         stacked = jnp.concatenate(
             [recv[d, s] for d in range(zs)]
-            + [jnp.concatenate(extras, 0).astype(jnp.bfloat16), last_buf[s]],
+            + extras + [last_buf[s]],
             0,
         )
         coef = jnp.dot(const[c0:c1, :inner], stacked, preferred_element_type=jnp.float32)
@@ -350,18 +373,24 @@
     for f in range(nf):
         g_re = jnp.where(lane_freq == f, real[f * nb : (f + 1) * nb], g_re)
         g_im = jnp.where(lane_freq == f, imag[f * nb : (f + 1) * nb], g_im)
-    z_part[0] = g_re * scale
-    z_part[1] = g_im * scale
+    group = FREQ_DEV * nb
+    lane = lax.broadcasted_iota(jnp.int32, (nb, side), 1)
+    packed = []
+    for z in range(zs):
+        re = pltpu.roll(g_re, (LANES - z * group) % LANES, 1) if z else g_re
+        im = pltpu.roll(g_im, (LANES + group - z * group) % LANES, 1) if z != 1 else g_im
+        packed.append(jnp.where(lane < group, re, jnp.where(lane < 2 * group, im, 0.0)) * scale)
+        z_part[z] = packed[z]
 
     z_copies = []
     for k in order:
         copy = pltpu.make_async_remote_copy(
-            z_part, z_recv.at[k], z_send_sem.at[k], z_recv_sem.at[k],
+            z_part.at[peers[k]], z_recv.at[k], z_send_sem.at[k], z_recv_sem.at[k],
             device_id=(my_s, peers[k]), device_id_type=MESH,
         )
         copy.start()
         z_copies.append(copy)
-    total = z_part[...]
+    total = z_part[my_z]
     for k, copy in zip(order, z_copies):
         copy.wait_recv()
         total = total + z_recv[k]
@@ -379,30 +408,24 @@
     total = s_recv[0]
     for d in range(1, ns):
         total = total + s_recv[d]
-    g_re, g_im = total[0], total[1]
+    g_re = jnp.where(lane < group, total, 0.0)
+    g_im = jnp.where(lane < group, pltpu.roll(total, LANES - group, 1), 0.0)
 
     value = leading_value(g_re, g_im, nb)
     row = lax.broadcasted_iota(jnp.int32, (nb, side), 0)
     mine = row == my_s
     row_re = jnp.sum(jnp.where(mine, g_re, 0.0), axis=0, keepdims=True)
     row_im = jnp.sum(jnp.where(mine, g_im, 0.0), axis=0, keepdims=True)
-    group = FREQ_DEV * nb
     result = jnp.where(row % 2 == 0, row_re, row_im)
-    placed, spread = result, value
-    for z in range(1, zs):
-        placed = jnp.where(my_z == z, pltpu.roll(result, LANES - z * group, 1), placed)
-        spread = jnp.where(my_z == z, pltpu.roll(value, LANES - z * group, 1), spread)
-    rows, values = placed, spread
-    lane = lax.broadcasted_iota(jnp.int32, (nb, side), 1)
+    rows, values = result, value
     for f in range(1, FREQ_DEV):
-        rows = jnp.where(row // 2 == f, pltpu.roll(placed, LANES - f * nb, 1), rows)
-        values = jnp.where(lane == f, pltpu.roll(spread, LANES - f * (nb - 1), 1), values)
+        rows = jnp.where(row // 2 == f, pltpu.roll(result, LANES - f * nb, 1), rows)
+        values = jnp.where(lane == f, pltpu.roll(value, LANES - f * (nb - 1), 1), values)
     gram_ref[...] = rows
     value_ref[...] = values
 
-    for group_copies in copies.values():
-        for copy in group_copies:
-            copy.wait_send()
+    for copy in copies.values():
+        copy.wait_send()
     for copy in z_copies + s_copies:
         copy.wait_send()
 
@@ -412,13 +435,13 @@
     nf = FREQ_DEV * zs
     nb = 2 * zs
     sub = points // zs // SUBS
-    pieces = sub // LANES
+    pieces = points // zs // LANES
     width = 2 * nf
-    table, tail_table = make_tables(nf, pieces)
+    table, ext_table, tail_table = make_tables(nf, pieces)
     combine = make_combine(nf, nb, pieces)
     window = 0.5 - 0.5 * np.cos(2.0 * np.pi * np.arange(NFFT) / NFFT)
     scale = float(1.0 / (points * ns * np.sum(window * window)))
-    parts = [table, tail_table, combine]
+    parts = [table, ext_table, tail_table, combine]
     inner = combine.shape[1]
     padded = -(-inner // LANES) * LANES
     const = np.concatenate([np.pad(p, ((0, 0), (0, padded - p.shape[1]))) for p in parts], 0)
@@ -437,14 +460,14 @@
             pltpu.VMEM((SUBS, tail_table.shape[0] // 2, sub), jnp.bfloat16),
             pltpu.VMEM(const.shape, jnp.bfloat16),
             pltpu.VMEM((zs, SUBS, 2 * width, sub), jnp.bfloat16),
-            pltpu.VMEM((zs, SUBS, 2 * pieces, LANES), jnp.float32),
+            pltpu.VMEM((zs, 2 * pieces, LANES), jnp.bfloat16),
             pltpu.VMEM((zs, SUBS, 2 * width, sub), jnp.bfloat16),
-            pltpu.VMEM((zs, SUBS, 2 * pieces, LANES), jnp.float32),
-            pltpu.VMEM((2, nb, LANES), jnp.float32),
-            pltpu.VMEM((zs, 2, nb, LANES), jnp.float32),
-            pltpu.VMEM((ns, 2, nb, LANES), jnp.float32),
+            pltpu.VMEM((zs, 2 * pieces, LANES), jnp.bfloat16),
+            pltpu.VMEM((zs, nb, LANES), jnp.float32),
+            pltpu.VMEM((zs, nb, LANES), jnp.float32),
+            pltpu.VMEM((ns, nb, LANES), jnp.float32),
             dma((zs, SUBS)), dma((4,)),
-            dma((zs, SUBS)), dma((zs, SUBS)), dma((zs, SUBS)), dma((zs, SUBS)),
+            dma((zs, SUBS)), dma((zs, SUBS)), dma((zs,)), dma((zs,)),
             dma((zs,)), dma((zs,)), dma((ns,)), dma((ns,)),
         ],
         compiler_params=pltpu.CompilerParams(

time: 30.2 us -> 29.7 us (0.983)
  Pallas kernels: 28.4 us -> 27.9 us
    pallas_call x1, Pallas kernels: 28.4 us -> 27.9 us  [shards_kernel(): pl.pallas_call(functools.partial(kernel, zs, ns, nf, nb, scale, spans, in...]
where the time goes in v6:
time: 29.7 us; the launch traced here: 29.6 us
  Pallas kernels  27.9 us (94%)
  local copies, waits for them, and re-layouts  1.11 us (4%)
  between operations  0.64 us (2%)
    pallas_call x1, Pallas kernels, shards_kernel(): pl.pallas_call(functools.partial(kernel, zs, ns, nf, nb, scale, spans, in...  27.9 us

profile of v6, /device:TPU:0, one launch (start us, length us, event | category | flops | bytes accessed | tf_op | source)
XLA Modules:
  0.0 29.6 jit_solution(17859956910303186094)
XLA Ops:
  0.6 27.9 %shard_map.50 = (f32[8,128]{1,0:T(8,128)S(1)}, f32[8,128]{1,0:T(8,128)S(1)}) custom-call(bf16[4096,256]{1,0:T(8,128)(2,1)} %snap_ref.1, bf16[4096,128]{1,0:T(8,128)(2,1)} %tail_ref.1, bf16[512,384]{1,0:T(8,128)(2,1)} %constant.2.clone.const_ref), custom_call_target="tpu_custom_call" | custom-call | flops 268435456 | bytes 2097152 | tf_op jit(solution)/shard_map/pallas_call | solution.py:452
  28.5 0.5 %slice_bitcast_fusion = f32[4]{0:T(128)} fusion(f32[8,128]{1,0:T(8,128)S(1)} %get-tuple-element.5), kind=kLoop, calls=%fused_computation | loop fusion | bytes 32 | tf_op jit(solution)/shard_map/squeeze | solution.py:480
  29.0 0.6 %copy.7 = f32[4,2,1,8]{3,2,1,0:T(1,128)} copy(f32[4,2,1,8]{3,2,1,0:T(1,128)S(1)} %bitcast.6) | data formatting | bytes 512

commit v7 on v6

--- a/solution.py
+++ b/solution.py
@@ -132,7 +132,7 @@
     last = np.zeros((width + 16, half))
     last[:width] = main
     last[width] = extra[0]
-    return two_pieces(both), two_pieces(extras), two_pieces(last)
+    return two_pieces(np.concatenate([both, extras], 0)), two_pieces(last)
 
 
 def make_combine(nf, nb, pieces):
@@ -253,10 +253,10 @@
         pl.semaphore_signal(barrier, inc=1, device_id=(friends[k], my_z), device_id_type=MESH)
 
     loads = {}
-    (t0, _), (e0, e1), (l0, l1), (c0, c1) = spans
+    (t0, t1), (l0, l1), (c0, c1) = spans
     constants = [
         pltpu.make_async_copy(const_ref.at[a:b], const.at[a:b], const_sem.at[i])
-        for i, (a, b) in enumerate([(t0, e1), (l0, l1), (c0, c1)])
+        for i, (a, b) in enumerate(spans)
     ] + [
         pltpu.make_async_copy(
             tail_ref.at[pl.ds(pl.multiple_of(my_z * quarter, quarter), quarter)],
@@ -280,15 +280,15 @@
         return x[:rows] + x[rows:]
 
     def transform(k, s):
-        return folded(nt_dot(const[t0:e0, : x_buf.shape[3]], x_buf[k, s])).astype(jnp.bfloat16)
-
-    def extras_of(k):
-        whole = x_buf[k].reshape(quarter, x_buf.shape[3])
-        rows = folded(nt_dot(const[e0:e1, : x_buf.shape[3]], whole))
-        extra = jnp.zeros((2 * pieces, LANES), jnp.float32)
-        for q in range(pieces):
-            extra = jnp.where(ext_row == q, rows[:, q * LANES : (q + 1) * LANES], extra)
-        return extra.astype(jnp.bfloat16)
+        loads[k, s].wait()
+        both = folded(nt_dot(const[t0:t1, : x_buf.shape[3]], x_buf[k, s]))
+        for q in range(here):
+            extras[k] = jnp.where(
+                ext_row == s * here + q,
+                both[2 * width :, q * LANES : (q + 1) * LANES],
+                extras[k],
+            )
+        return both[: 2 * width].astype(jnp.bfloat16)
 
     def started(source, target, send_sems, recv_sems, k):
         copy = pltpu.make_async_remote_copy(
@@ -300,16 +300,19 @@
 
     constants[0].wait()
     copies = {}
-    for s in range(SUBS):
+    extras = {k: jnp.zeros((2 * pieces, LANES), jnp.float32) for k in [0] + order}
+
+    def send_main(k, s):
+        copies[k, s] = started(
+            send.at[k, s], recv.at[my_z, s], send_sem.at[k, s], recv_sem.at[k, s], k
+        )
+
+    for s in range(SUBS - 1):
         for k in order:
-            if s < 2:
-                loads[k, s].wait()
             send[k, s] = transform(k, s)
             if s == 0 and k == order[0]:
                 pl.semaphore_wait(barrier, zs - 1 + ns - 1)
-            copies[k, s] = started(
-                send.at[k, s], recv.at[my_z, s], send_sem.at[k, s], recv_sem.at[k, s], k
-            )
+            send_main(k, s)
             if s == 0 and k == order[0]:
                 for later in range(1, SUBS):
                     for i in order:
@@ -318,18 +321,17 @@
                     loads[0, i].start()
                 for copy in constants[1:]:
                     copy.start()
-        if s == 1:
-            for k in order:
-                for later in range(2, SUBS):
-                    loads[k, later].wait()
-                send_ext[k] = extras_of(k)
-                copies[k, "ext"] = started(
-                    send_ext.at[k], recv_ext.at[my_z], ext_send_sem.at[k], ext_recv_sem.at[k], k
-                )
+    for k in order:
+        send[k, SUBS - 1] = transform(k, SUBS - 1)
+        send_ext[k] = extras[k].astype(jnp.bfloat16)
+        copies[k, "ext"] = started(
+            send_ext.at[k], recv_ext.at[my_z], ext_send_sem.at[k], ext_recv_sem.at[k], k
+        )
+    for k in order:
+        send_main(k, SUBS - 1)
     for s in range(SUBS):
-        loads[0, s].wait()
         recv[my_z, s] = transform(0, s)
-    recv_ext[my_z] = extras_of(0)
+    recv_ext[my_z] = extras[0].astype(jnp.bfloat16)
     for copy in constants[1:]:
         copy.wait()
     for s in range(SUBS):
@@ -343,10 +345,10 @@
             copies[k, s].wait_recv()
             if s == 0:
                 copies[k, "ext"].wait_recv()
-        extras = []
+        spread = []
         for d in range(zs):
             extra = recv_ext[d]
-            extras.append(
+            spread.append(
                 jnp.concatenate(
                     [
                         jnp.where(ext_row == s * here + q, extra, jnp.zeros_like(extra))
@@ -357,7 +359,7 @@
             )
         stacked = jnp.concatenate(
             [recv[d, s] for d in range(zs)]
-            + extras + [last_buf[s]],
+            + spread + [last_buf[s]],
             0,
         )
         coef = jnp.dot(const[c0:c1, :inner], stacked, preferred_element_type=jnp.float32)
@@ -437,11 +439,11 @@
     sub = points // zs // SUBS
     pieces = points // zs // LANES
     width = 2 * nf
-    table, ext_table, tail_table = make_tables(nf, pieces)
+    table, tail_table = make_tables(nf, pieces)
     combine = make_combine(nf, nb, pieces)
     window = 0.5 - 0.5 * np.cos(2.0 * np.pi * np.arange(NFFT) / NFFT)
     scale = float(1.0 / (points * ns * np.sum(window * window)))
-    parts = [table, ext_table, tail_table, combine]
+    parts = [table, tail_table, combine]
     inner = combine.shape[1]
     padded = -(-inner // LANES) * LANES
     const = np.concatenate([np.pad(p, ((0, 0), (0, padded - p.shape[1]))) for p in parts], 0)

time: 29.7 us -> 30.4 us (1.024)
  Pallas kernels: 27.9 us -> 28.5 us
    pallas_call x1, Pallas kernels: 27.9 us -> 28.5 us  [shards_kernel(): pl.pallas_call(functools.partial(kernel, zs, ns, nf, nb, scale, spans, in...]
where the time goes in v7:
time: 30.4 us; the launch traced here: 30.2 us
  Pallas kernels  28.5 us (94%)
  local copies, waits for them, and re-layouts  1.11 us (4%)
  between operations  0.64 us (2%)
    pallas_call x1, Pallas kernels, shards_kernel(): pl.pallas_call(functools.partial(kernel, zs, ns, nf, nb, scale, spans, in...  28.5 us

profile of v7, /device:TPU:0, one launch (start us, length us, event | category | flops | bytes accessed | tf_op | source)
XLA Modules:
  0.0 30.2 jit_solution(9135668551464070420)
XLA Ops:
  0.6 28.5 %shard_map.50 = (f32[8,128]{1,0:T(8,128)S(1)}, f32[8,128]{1,0:T(8,128)S(1)}) custom-call(bf16[4096,256]{1,0:T(8,128)(2,1)} %snap_ref.1, bf16[4096,128]{1,0:T(8,128)(2,1)} %tail_ref.1, bf16[512,384]{1,0:T(8,128)(2,1)} %constant.2.clone.const_ref), custom_call_target="tpu_custom_call" | custom-call | flops 335544320 | bytes 2097152 | tf_op jit(solution)/shard_map/pallas_call | solution.py:454
  29.1 0.5 %slice_bitcast_fusion = f32[4]{0:T(128)} fusion(f32[8,128]{1,0:T(8,128)S(1)} %get-tuple-element.5), kind=kLoop, calls=%fused_computation | loop fusion | bytes 32 | tf_op jit(solution)/shard_map/squeeze | solution.py:482
  29.6 0.6 %copy.7 = f32[4,2,1,8]{3,2,1,0:T(1,128)} copy(f32[4,2,1,8]{3,2,1,0:T(1,128)S(1)} %bitcast.6) | data formatting | bytes 512

commit v8 on v6

--- a/solution.py
+++ b/solution.py
@@ -337,11 +337,11 @@
         rows = last.shape[0] // 2
         last_buf[s] = (last[:rows] + last[rows:]).astype(jnp.bfloat16)
 
+    main_rows = nb * width
     gram = jnp.zeros((width * nb, width * nb), jnp.float32)
     for s in range(SUBS):
-        for k in order:
-            copies[k, s].wait_recv()
-            if s == 0:
+        if s == 0:
+            for k in order:
                 copies[k, "ext"].wait_recv()
         extras = []
         for d in range(zs):
@@ -355,12 +355,17 @@
                     1,
                 )
             )
-        stacked = jnp.concatenate(
-            [recv[d, s] for d in range(zs)]
-            + extras + [last_buf[s]],
-            0,
+        rest = jnp.dot(
+            const[c0:c1, main_rows:inner],
+            jnp.concatenate(extras + [last_buf[s]], 0),
+            preferred_element_type=jnp.float32,
         )
-        coef = jnp.dot(const[c0:c1, :inner], stacked, preferred_element_type=jnp.float32)
+        for k in order:
+            copies[k, s].wait_recv()
+        stacked = jnp.concatenate([recv[d, s] for d in range(zs)], 0)
+        coef = rest + jnp.dot(
+            const[c0:c1, :main_rows], stacked, preferred_element_type=jnp.float32
+        )
         coef = coef.astype(jnp.bfloat16)
         gram = gram + nt_dot(coef, coef)
 

time: 29.7 us -> 29.7 us (level)
  no operation moved by 1% of the time
where the time goes in v8:
time: 29.7 us; the launch traced here: 29.6 us
  Pallas kernels  27.9 us (94%)
  local copies, waits for them, and re-layouts  1.11 us (4%)
  between operations  0.64 us (2%)
    pallas_call x1, Pallas kernels, shards_kernel(): pl.pallas_call(functools.partial(kernel, zs, ns, nf, nb, scale, spans, in...  27.9 us

profile of v8, /device:TPU:0, one launch (start us, length us, event | category | flops | bytes accessed | tf_op | source)
XLA Modules:
  0.0 29.6 jit_solution(17644345461444020956)
XLA Ops:
  0.6 27.9 %shard_map.50 = (f32[8,128]{1,0:T(8,128)S(1)}, f32[8,128]{1,0:T(8,128)S(1)}) custom-call(bf16[4096,256]{1,0:T(8,128)(2,1)} %snap_ref.1, bf16[4096,128]{1,0:T(8,128)(2,1)} %tail_ref.1, bf16[512,384]{1,0:T(8,128)(2,1)} %constant.2.clone.const_ref), custom_call_target="tpu_custom_call" | custom-call | flops 268435456 | bytes 2097152 | tf_op jit(solution)/shard_map/pallas_call | solution.py:457
  28.5 0.5 %slice_bitcast_fusion = f32[4]{0:T(128)} fusion(f32[8,128]{1,0:T(8,128)S(1)} %get-tuple-element.5), kind=kLoop, calls=%fused_computation | loop fusion | bytes 32 | tf_op jit(solution)/shard_map/squeeze | solution.py:485
  29.0 0.6 %copy.7 = f32[4,2,1,8]{3,2,1,0:T(1,128)} copy(f32[4,2,1,8]{3,2,1,0:T(1,128)S(1)} %bitcast.6) | data formatting | bytes 512

commit v9 on v8

--- a/solution.py
+++ b/solution.py
@@ -433,6 +433,11 @@
         copy.wait_send()
     for copy in z_copies + s_copies:
         copy.wait_send()
+
+
+def place_results(gram_ref, value_ref, rows_ref, top_ref):
+    rows_ref[...] = gram_ref[:, : rows_ref.shape[1]]
+    top_ref[...] = value_ref[0:1, : top_ref.shape[1]]
 
 
 def shards_kernel(zs, ns, snapshots, tail):
@@ -482,7 +487,16 @@
             flops=flops, bytes_accessed=points * steps * 2, transcendentals=0
         ),
     )(snapshots, tail, jnp.asarray(const))
-    return gram[:, :nb].reshape(FREQ_DEV, 2, 1, nb), values[0, :FREQ_DEV]
+    rows, top = pl.pallas_call(
+        place_results,
+        out_shape=[
+            jax.ShapeDtypeStruct((2 * FREQ_DEV, nb), jnp.float32),
+            jax.ShapeDtypeStruct((1, FREQ_DEV), jnp.float32),
+        ],
+        in_specs=[pl.BlockSpec(memory_space=pltpu.VMEM)] * 2,
+        out_specs=[pl.BlockSpec(memory_space=pltpu.VMEM)] * 2,
+    )(gram, values)
+    return rows.reshape(FREQ_DEV, 2, 1, nb), top.reshape(FREQ_DEV)
 
 
 def power_of_two(count):

time: 29.7 us -> 31.1 us (1.047)
  Pallas kernels: 27.9 us -> 29.1 us
    pallas_call x0 -> x1, Pallas kernels: none -> 1.28 us  [shards_kernel(): pl.pallas_call(place_results, out_shape=[jax.ShapeDtypeStruct((2 * FREQ_D...]
    unnamed x1 -> x4, local copies, waits for them, and re-layouts: 0.59 us -> 1.17 us
    squeeze x1 -> x0, local copies, waits for them, and re-layouts: 0.51 us -> none  [shards_kernel(): return (gram[:, :nb].reshape(FREQ_DEV, 2, 1, nb), values[0, :FREQ_DEV])]
where the time goes in v9:
time: 31.1 us; the launch traced here: 30.9 us
  Pallas kernels  29.1 us (94%)
  local copies, waits for them, and re-layouts  1.17 us (4%)
  between operations  0.65 us (2%)
    pallas_call x1, Pallas kernels, shards_kernel(): pl.pallas_call(functools.partial(kernel, zs, ns, nf, nb, scale, spans, in...  27.9 us
    pallas_call x1, Pallas kernels, shards_kernel(): pl.pallas_call(place_results, out_shape=[jax.ShapeDtypeStruct((2 * FREQ_D...  1.28 us
    unnamed x4, local copies, waits for them, and re-layouts  1.17 us

profile of v9, /device:TPU:0, one launch (start us, length us, event | category | flops | bytes accessed | tf_op | source)
XLA Modules:
  0.0 30.9 jit_solution(12497768630757483574)
XLA Ops:
  0.6 27.9 %shard_map.50 = (f32[8,128]{1,0:T(8,128)S(1)}, f32[8,128]{1,0:T(8,128)S(1)}) custom-call(bf16[4096,256]{1,0:T(8,128)(2,1)} %snap_ref.1, bf16[4096,128]{1,0:T(8,128)(2,1)} %tail_ref.1, bf16[512,384]{1,0:T(8,128)(2,1)} %constant.2.clone.const_ref), custom_call_target="tpu_custom_call" | custom-call | flops 268435456 | bytes 2097152 | tf_op jit(solution)/shard_map/pallas_call | solution.py:462
  28.5 0.0 copy-start
  28.5 0.6 %copy-done = f32[8,128]{1,0:T(8,128)} copy-done((f32[8,128]{1,0:T(8,128)}, f32[8,128]{1,0:T(8,128)S(1)}, u32[]{:S(2)}) %copy-start) | copy-done | bytes 4120
  29.1 0.0 copy-start.1
  29.1 0.6 %copy-done.1 = f32[8,128]{1,0:T(8,128)} copy-done((f32[8,128]{1,0:T(8,128)}, f32[8,128]{1,0:T(8,128)S(1)}, u32[]{:S(2)}) %copy-start.1) | copy-done | bytes 4120
  29.7 1.3 %shard_map.51 = (f32[8,8]{1,0:T(8,128)}, f32[1,4]{1,0:T(1,128)}) custom-call(f32[8,128]{1,0:T(8,128)} %copy-done, f32[8,128]{1,0:T(8,128)} %copy-done.1), custom_call_target="tpu_custom_call" | custom-call | tf_op jit(solution)/shard_map/pallas_call | solution.py:490
Async XLA Ops:
  28.5 0.6 %copy-start = (f32[8,128]{1,0:T(8,128)}, f32[8,128]{1,0:T(8,128)S(1)}, u32[]{:S(2)}) copy-start(f32[8,128]{1,0:T(8,128)S(1)} %get-tuple-element.6.gram_ref) | copy-start | bytes 12292
  29.1 0.6 %copy-start.1 = (f32[8,128]{1,0:T(8,128)}, f32[8,128]{1,0:T(8,128)S(1)}, u32[]{:S(2)}) copy-start(f32[8,128]{1,0:T(8,128)S(1)} %get-tuple-element.7.value_ref) | copy-start | bytes 12292

commit v10 on v8

--- a/solution.py
+++ b/solution.py
@@ -14,7 +14,7 @@
 NFFT = 256
 POWER = 4
 LANES = 128
-SUBS = 4
+SUBS = 8
 MESH = pl.DeviceIdType.MESH
 
 

time: 29.7 us -> 30.6 us (1.030)
  Pallas kernels: 27.9 us -> 28.7 us
    pallas_call x1, Pallas kernels: 27.9 us -> 28.7 us  [shards_kernel(): pl.pallas_call(functools.partial(kernel, zs, ns, nf, nb, scale, spans, in...]
where the time goes in v10:
time: 30.6 us; the launch traced here: 30.5 us
  Pallas kernels  28.7 us (94%)
  local copies, waits for them, and re-layouts  1.11 us (4%)
  between operations  0.64 us (2%)
    pallas_call x1, Pallas kernels, shards_kernel(): pl.pallas_call(functools.partial(kernel, zs, ns, nf, nb, scale, spans, in...  28.7 us

profile of v10, /device:TPU:0, one launch (start us, length us, event | category | flops | bytes accessed | tf_op | source)
XLA Modules:
  0.0 30.5 jit_solution(15055031385553660518)
XLA Ops:
  0.6 28.7 %shard_map.50 = (f32[8,128]{1,0:T(8,128)S(1)}, f32[8,128]{1,0:T(8,128)S(1)}) custom-call(bf16[4096,256]{1,0:T(8,128)(2,1)} %snap_ref.1, bf16[4096,128]{1,0:T(8,128)(2,1)} %tail_ref.1, bf16[512,384]{1,0:T(8,128)(2,1)} %constant.2.clone.const_ref), custom_call_target="tpu_custom_call" | custom-call | flops 268435456 | bytes 2097152 | tf_op jit(solution)/shard_map/pallas_call | solution.py:457
  29.4 0.5 %slice_bitcast_fusion = f32[4]{0:T(128)} fusion(f32[8,128]{1,0:T(8,128)S(1)} %get-tuple-element.5), kind=kLoop, calls=%fused_computation | loop fusion | bytes 32 | tf_op jit(solution)/shard_map/squeeze | solution.py:485
  29.9 0.6 %copy.7 = f32[4,2,1,8]{3,2,1,0:T(1,128)} copy(f32[4,2,1,8]{3,2,1,0:T(1,128)S(1)} %bitcast.6) | data formatting | bytes 512
